TPU v7x, 32 devices: a whole 2x2x4 slice. The times are simulated.
32 devices in a mesh: ind: 8 (over z, x), snp: 4 (over y, core).
Axes of the slice: x: 2, y: 2, z: 4, core: 2. Of those that a mesh axis runs over, the one named last changes fastest.
Arguments:
- genotype: int32 [4096, 8192], P('ind', 'snp'), may hold values from 0 to 170, as said below
- probe: bfloat16 [24, 8192], P(None, 'snp'), may hold values from -0.0625 to 0.0625
- allele_mean: float32 [8192], P('snp'), may hold values from 0.2 to 1.8
- allele_scale: float32 [8192], P('snp'), may hold values from 0.3 to 3
Outputs:
- projected: float32 [24, 8192], P(None, 'snp')
Inputs may be any that keep to these rules, and one draw needn't show every extreme that they name: `genotype`: word r of a column holds the codes of individuals 4 r + k, k = 0 to 3, in bits 2 k and 2 k + 1; every code is 0, 1 or 2.
All inputs are finite; a program needn't handle non-finite values.
Results may differ from a plain program's by a relative error of at most 0.0095.
Values may be sent and summed in bfloat16 or wider, within the bound.
A program may use at most 64 MiB of HBM per device.

v0:
```python
import math

import jax
import jax.numpy as jnp
from jax import lax
from jax.sharding import PartitionSpec as P


def unpack(packed, allele_mean, allele_scale):
    planes = []
    for offset in range(4):
        codes = jnp.bitwise_and(jnp.right_shift(packed, 2 * offset), 3)
        planes.append(
            ((codes.astype(jnp.float32) - allele_mean) * allele_scale).astype(jnp.bfloat16)
        )
    stacked = jnp.stack(planes, axis=1)
    return stacked.reshape(packed.shape[0] * 4, packed.shape[1])


def sketch_rows(genotype, probe, allele_mean, allele_scale):
    word_rows = genotype.shape[0]
    block_words = math.gcd(word_rows, 32)
    blocks = genotype.reshape(word_rows // block_words, block_words, genotype.shape[1])

    def one_block(packed):
        zed = unpack(packed, allele_mean, allele_scale)
        return lax.dot_general(
            probe, zed, (((1,), (1,)), ((), ())), preferred_element_type=jnp.float32
        )

    pieces = lax.map(one_block, blocks)
    return pieces.transpose(1, 0, 2).reshape(probe.shape[0], word_rows * 4)


def project_rows(packed_rows, basis_cols, allele_mean, allele_scale):
    word_rows = packed_rows.shape[0]
    block_words = math.gcd(word_rows, 32)
    block_count = word_rows // block_words
    blocks = packed_rows.reshape(block_count, block_words, packed_rows.shape[1])
    basis_blocks = basis_cols.reshape(basis_cols.shape[0], block_count, 4 * block_words).transpose(
        1, 0, 2
    )

    def step_block(total, inputs):
        packed, basis_block = inputs
        zed = unpack(packed, allele_mean, allele_scale)
        return (total + jnp.dot(basis_block, zed, preferred_element_type=jnp.float32), 0.0)

    start_total = jnp.zeros((basis_cols.shape[0], packed_rows.shape[1]), jnp.float32)
    total, ignored = lax.scan(step_block, start_total, (blocks, basis_blocks))
    return total


def on_device(genotype, probe, allele_mean, allele_scale):
    partial_sketch = sketch_rows(genotype, probe, allele_mean, allele_scale)
    slice_rows = lax.psum_scatter(
        partial_sketch.astype(jnp.bfloat16), "snp", scatter_dimension=1, tiled=True
    ).astype(jnp.float32)
    gram = jnp.dot(
        slice_rows,
        slice_rows.T,
        precision=lax.Precision.HIGHEST,
        preferred_element_type=jnp.float32,
    )
    total = lax.psum(gram, ("ind", "snp"))
    lower = jnp.linalg.cholesky(total)
    basis_slice = jax.scipy.linalg.solve_triangular(lower, slice_rows, lower=True).astype(
        jnp.bfloat16
    )
    product = project_rows(
        genotype, lax.all_gather(basis_slice, "snp", axis=1, tiled=True), allele_mean, allele_scale
    )
    return lax.psum(product.astype(jnp.bfloat16), "ind").astype(jnp.float32)


def solution(mesh):
    in_specs = (P("ind", "snp"), P(None, "snp"), P("snp"), P("snp"))
    out_specs = P(None, "snp")
    return jax.shard_map(
        on_device, mesh=mesh, in_specs=in_specs, out_specs=out_specs, check_vma=False
    )
```

profile of v0, /device:TPU:0, one launch (start us, length us, event | category | flops | bytes accessed | tf_op | source)
XLA Modules:
  0.0 324.9 jit_solution(439660619284668419)
XLA Ops:
  6.5 6.6 %copy.12 = s32[16,32,2048]{2,0,1:T(8,128)} copy(s32[16,32,2048]{2,1,0:T(8,128)} %bitcast.102) | data formatting | bytes 8388608 | tf_op jit(solution)/shard_map/while | solution.py:31
  13.1 78.9 %while.21 = (s32[]{:T(128)}, bf16[16,24,128]{2,1,0:T(8,128)(2,1)S(1)}, s32[16,32,2048]{2,0,1:T(8,128)}, f32[2048]{0:T(1024)S(1)}, f32[2048]{0:T(1024)S(1)}, /*index=5*/bf16[24,2048]{1,0:T(8,128)(2,1)S(1)}, s32[]{:T(128)}) while((s32[]{:T(128)}, bf16[16,24,128]{2,1,0:T(8,128)(2,1)S(1)}, s32[16,32,2048]{2,0,1:T(8,128)}, f32[2048]{0:T(1024)S(1)}, ...), condition=%wide.region_1.2_spmd, body=%wide.region_0.1_spmd.sunk | while | flops 16252930 | bytes 3534933 | solution.py:31
  13.1 3.3 %fusion.41 = (bf16[32,1,2048]{2,1,0:T(2,128)(2,1)S(1)}, bf16[32,1,2048]{2,1,0:T(2,128)(2,1)S(1)}, bf16[32,1,2048]{2,1,0:T(2,128)(2,1)S(1)}, bf16[32,1,2048]{2,1,0:T(2,128)(2,1)S(1)}) fusion(f32[2048]{0:T(1024)S(1)} %get-tuple-element.244, f32[2048]{0:T(1024)S(1)} %get-tuple-element.243, s32[16,32,2048]{2,0,1:T(8,128)} %get-tuple-element.242, ...), kind=kLoop, calls=%fused_computation.14.clone.1 | loop fusion | flops 1572864 | bytes 802820 | tf_op jit(solution)/shard_map/while/body/eval_jaxpr/convert_element_type | solution.py:14
  18.1 3.3 %fusion.41 = (bf16[32,1,2048]{2,1,0:T(2,128)(2,1)S(1)}, bf16[32,1,2048]{2,1,0:T(2,128)(2,1)S(1)}, bf16[32,1,2048]{2,1,0:T(2,128)(2,1)S(1)}, bf16[32,1,2048]{2,1,0:T(2,128)(2,1)S(1)}) fusion(f32[2048]{0:T(1024)S(1)} %get-tuple-element.244, f32[2048]{0:T(1024)S(1)} %get-tuple-element.243, s32[16,32,2048]{2,0,1:T(8,128)} %get-tuple-element.242, ...), kind=kLoop, calls=%fused_computation.14.clone.1 | loop fusion | flops 1572864 | bytes 802820 | tf_op jit(solution)/shard_map/while/body/eval_jaxpr/convert_element_type | solution.py:14
  23.0 3.3 %fusion.41 = (bf16[32,1,2048]{2,1,0:T(2,128)(2,1)S(1)}, bf16[32,1,2048]{2,1,0:T(2,128)(2,1)S(1)}, bf16[32,1,2048]{2,1,0:T(2,128)(2,1)S(1)}, bf16[32,1,2048]{2,1,0:T(2,128)(2,1)S(1)}) fusion(f32[2048]{0:T(1024)S(1)} %get-tuple-element.244, f32[2048]{0:T(1024)S(1)} %get-tuple-element.243, s32[16,32,2048]{2,0,1:T(8,128)} %get-tuple-element.242, ...), kind=kLoop, calls=%fused_computation.14.clone.1 | loop fusion | flops 1572864 | bytes 802820 | tf_op jit(solution)/shard_map/while/body/eval_jaxpr/convert_element_type | solution.py:14
  27.9 3.3 %fusion.41 = (bf16[32,1,2048]{2,1,0:T(2,128)(2,1)S(1)}, bf16[32,1,2048]{2,1,0:T(2,128)(2,1)S(1)}, bf16[32,1,2048]{2,1,0:T(2,128)(2,1)S(1)}, bf16[32,1,2048]{2,1,0:T(2,128)(2,1)S(1)}) fusion(f32[2048]{0:T(1024)S(1)} %get-tuple-element.244, f32[2048]{0:T(1024)S(1)} %get-tuple-element.243, s32[16,32,2048]{2,0,1:T(8,128)} %get-tuple-element.242, ...), kind=kLoop, calls=%fused_computation.14.clone.1 | loop fusion | flops 1572864 | bytes 802820 | tf_op jit(solution)/shard_map/while/body/eval_jaxpr/convert_element_type | solution.py:14
  32.9 3.3 %fusion.41 = (bf16[32,1,2048]{2,1,0:T(2,128)(2,1)S(1)}, bf16[32,1,2048]{2,1,0:T(2,128)(2,1)S(1)}, bf16[32,1,2048]{2,1,0:T(2,128)(2,1)S(1)}, bf16[32,1,2048]{2,1,0:T(2,128)(2,1)S(1)}) fusion(f32[2048]{0:T(1024)S(1)} %get-tuple-element.244, f32[2048]{0:T(1024)S(1)} %get-tuple-element.243, s32[16,32,2048]{2,0,1:T(8,128)} %get-tuple-element.242, ...), kind=kLoop, calls=%fused_computation.14.clone.1 | loop fusion | flops 1572864 | bytes 802820 | tf_op jit(solution)/shard_map/while/body/eval_jaxpr/convert_element_type | solution.py:14
  37.8 3.3 %fusion.41 = (bf16[32,1,2048]{2,1,0:T(2,128)(2,1)S(1)}, bf16[32,1,2048]{2,1,0:T(2,128)(2,1)S(1)}, bf16[32,1,2048]{2,1,0:T(2,128)(2,1)S(1)}, bf16[32,1,2048]{2,1,0:T(2,128)(2,1)S(1)}) fusion(f32[2048]{0:T(1024)S(1)} %get-tuple-element.244, f32[2048]{0:T(1024)S(1)} %get-tuple-element.243, s32[16,32,2048]{2,0,1:T(8,128)} %get-tuple-element.242, ...), kind=kLoop, calls=%fused_computation.14.clone.1 | loop fusion | flops 1572864 | bytes 802820 | tf_op jit(solution)/shard_map/while/body/eval_jaxpr/convert_element_type | solution.py:14
  42.7 3.3 %fusion.41 = (bf16[32,1,2048]{2,1,0:T(2,128)(2,1)S(1)}, bf16[32,1,2048]{2,1,0:T(2,128)(2,1)S(1)}, bf16[32,1,2048]{2,1,0:T(2,128)(2,1)S(1)}, bf16[32,1,2048]{2,1,0:T(2,128)(2,1)S(1)}) fusion(f32[2048]{0:T(1024)S(1)} %get-tuple-element.244, f32[2048]{0:T(1024)S(1)} %get-tuple-element.243, s32[16,32,2048]{2,0,1:T(8,128)} %get-tuple-element.242, ...), kind=kLoop, calls=%fused_computation.14.clone.1 | loop fusion | flops 1572864 | bytes 802820 | tf_op jit(solution)/shard_map/while/body/eval_jaxpr/convert_element_type | solution.py:14
  47.7 3.3 %fusion.41 = (bf16[32,1,2048]{2,1,0:T(2,128)(2,1)S(1)}, bf16[32,1,2048]{2,1,0:T(2,128)(2,1)S(1)}, bf16[32,1,2048]{2,1,0:T(2,128)(2,1)S(1)}, bf16[32,1,2048]{2,1,0:T(2,128)(2,1)S(1)}) fusion(f32[2048]{0:T(1024)S(1)} %get-tuple-element.244, f32[2048]{0:T(1024)S(1)} %get-tuple-element.243, s32[16,32,2048]{2,0,1:T(8,128)} %get-tuple-element.242, ...), kind=kLoop, calls=%fused_computation.14.clone.1 | loop fusion | flops 1572864 | bytes 802820 | tf_op jit(solution)/shard_map/while/body/eval_jaxpr/convert_element_type | solution.py:14
  52.6 3.3 %fusion.41 = (bf16[32,1,2048]{2,1,0:T(2,128)(2,1)S(1)}, bf16[32,1,2048]{2,1,0:T(2,128)(2,1)S(1)}, bf16[32,1,2048]{2,1,0:T(2,128)(2,1)S(1)}, bf16[32,1,2048]{2,1,0:T(2,128)(2,1)S(1)}) fusion(f32[2048]{0:T(1024)S(1)} %get-tuple-element.244, f32[2048]{0:T(1024)S(1)} %get-tuple-element.243, s32[16,32,2048]{2,0,1:T(8,128)} %get-tuple-element.242, ...), kind=kLoop, calls=%fused_computation.14.clone.1 | loop fusion | flops 1572864 | bytes 802820 | tf_op jit(solution)/shard_map/while/body/eval_jaxpr/convert_element_type | solution.py:14
  57.5 3.3 %fusion.41 = (bf16[32,1,2048]{2,1,0:T(2,128)(2,1)S(1)}, bf16[32,1,2048]{2,1,0:T(2,128)(2,1)S(1)}, bf16[32,1,2048]{2,1,0:T(2,128)(2,1)S(1)}, bf16[32,1,2048]{2,1,0:T(2,128)(2,1)S(1)}) fusion(f32[2048]{0:T(1024)S(1)} %get-tuple-element.244, f32[2048]{0:T(1024)S(1)} %get-tuple-element.243, s32[16,32,2048]{2,0,1:T(8,128)} %get-tuple-element.242, ...), kind=kLoop, calls=%fused_computation.14.clone.1 | loop fusion | flops 1572864 | bytes 802820 | tf_op jit(solution)/shard_map/while/body/eval_jaxpr/convert_element_type | solution.py:14
  62.5 3.3 %fusion.41 = (bf16[32,1,2048]{2,1,0:T(2,128)(2,1)S(1)}, bf16[32,1,2048]{2,1,0:T(2,128)(2,1)S(1)}, bf16[32,1,2048]{2,1,0:T(2,128)(2,1)S(1)}, bf16[32,1,2048]{2,1,0:T(2,128)(2,1)S(1)}) fusion(f32[2048]{0:T(1024)S(1)} %get-tuple-element.244, f32[2048]{0:T(1024)S(1)} %get-tuple-element.243, s32[16,32,2048]{2,0,1:T(8,128)} %get-tuple-element.242, ...), kind=kLoop, calls=%fused_computation.14.clone.1 | loop fusion | flops 1572864 | bytes 802820 | tf_op jit(solution)/shard_map/while/body/eval_jaxpr/convert_element_type | solution.py:14
  67.4 3.3 %fusion.41 = (bf16[32,1,2048]{2,1,0:T(2,128)(2,1)S(1)}, bf16[32,1,2048]{2,1,0:T(2,128)(2,1)S(1)}, bf16[32,1,2048]{2,1,0:T(2,128)(2,1)S(1)}, bf16[32,1,2048]{2,1,0:T(2,128)(2,1)S(1)}) fusion(f32[2048]{0:T(1024)S(1)} %get-tuple-element.244, f32[2048]{0:T(1024)S(1)} %get-tuple-element.243, s32[16,32,2048]{2,0,1:T(8,128)} %get-tuple-element.242, ...), kind=kLoop, calls=%fused_computation.14.clone.1 | loop fusion | flops 1572864 | bytes 802820 | tf_op jit(solution)/shard_map/while/body/eval_jaxpr/convert_element_type | solution.py:14
  72.3 3.3 %fusion.41 = (bf16[32,1,2048]{2,1,0:T(2,128)(2,1)S(1)}, bf16[32,1,2048]{2,1,0:T(2,128)(2,1)S(1)}, bf16[32,1,2048]{2,1,0:T(2,128)(2,1)S(1)}, bf16[32,1,2048]{2,1,0:T(2,128)(2,1)S(1)}) fusion(f32[2048]{0:T(1024)S(1)} %get-tuple-element.244, f32[2048]{0:T(1024)S(1)} %get-tuple-element.243, s32[16,32,2048]{2,0,1:T(8,128)} %get-tuple-element.242, ...), kind=kLoop, calls=%fused_computation.14.clone.1 | loop fusion | flops 1572864 | bytes 802820 | tf_op jit(solution)/shard_map/while/body/eval_jaxpr/convert_element_type | solution.py:14
  77.3 3.3 %fusion.41 = (bf16[32,1,2048]{2,1,0:T(2,128)(2,1)S(1)}, bf16[32,1,2048]{2,1,0:T(2,128)(2,1)S(1)}, bf16[32,1,2048]{2,1,0:T(2,128)(2,1)S(1)}, bf16[32,1,2048]{2,1,0:T(2,128)(2,1)S(1)}) fusion(f32[2048]{0:T(1024)S(1)} %get-tuple-element.244, f32[2048]{0:T(1024)S(1)} %get-tuple-element.243, s32[16,32,2048]{2,0,1:T(8,128)} %get-tuple-element.242, ...), kind=kLoop, calls=%fused_computation.14.clone.1 | loop fusion | flops 1572864 | bytes 802820 | tf_op jit(solution)/shard_map/while/body/eval_jaxpr/convert_element_type | solution.py:14
  82.2 3.3 %fusion.41 = (bf16[32,1,2048]{2,1,0:T(2,128)(2,1)S(1)}, bf16[32,1,2048]{2,1,0:T(2,128)(2,1)S(1)}, bf16[32,1,2048]{2,1,0:T(2,128)(2,1)S(1)}, bf16[32,1,2048]{2,1,0:T(2,128)(2,1)S(1)}) fusion(f32[2048]{0:T(1024)S(1)} %get-tuple-element.244, f32[2048]{0:T(1024)S(1)} %get-tuple-element.243, s32[16,32,2048]{2,0,1:T(8,128)} %get-tuple-element.242, ...), kind=kLoop, calls=%fused_computation.14.clone.1 | loop fusion | flops 1572864 | bytes 802820 | tf_op jit(solution)/shard_map/while/body/eval_jaxpr/convert_element_type | solution.py:14
  87.1 3.3 %fusion.41 = (bf16[32,1,2048]{2,1,0:T(2,128)(2,1)S(1)}, bf16[32,1,2048]{2,1,0:T(2,128)(2,1)S(1)}, bf16[32,1,2048]{2,1,0:T(2,128)(2,1)S(1)}, bf16[32,1,2048]{2,1,0:T(2,128)(2,1)S(1)}) fusion(f32[2048]{0:T(1024)S(1)} %get-tuple-element.244, f32[2048]{0:T(1024)S(1)} %get-tuple-element.243, s32[16,32,2048]{2,0,1:T(8,128)} %get-tuple-element.242, ...), kind=kLoop, calls=%fused_computation.14.clone.1 | loop fusion | flops 1572864 | bytes 802820 | tf_op jit(solution)/shard_map/while/body/eval_jaxpr/convert_element_type | solution.py:14
  92.8 22.3 %reduce-scatter.2.cloned.1.call-done = bf16[24,512]{1,0:T(8,128)(2,1)} async-done(((bf16[24,2048]{1,0:T(8,128)(2,1)}), bf16[24,512]{1,0:T(8,128)(2,1)}) %reduce-scatter.2.cloned.1.call-update) | async-done | bytes 24592 | tf_op jit(solution)/shard_map/reduce_scatter | solution.py:56
  116.1 39.4 %psum.14 = f32[24,24]{0,1:T(8,128)S(1)} all-reduce(f32[24,24]{0,1:T(8,128)S(1)} %fusion.23), channel_id=1, replica_groups=mesh['ind'=8,'snp'=4] {'ind','snp'}, use_global_device_ids=true, to_apply=%region_3.4 | all-reduce | flops 576 | bytes 4608 | tf_op jit(solution)/shard_map/psum | solution.py:65
  161.9 5.7 %all_gather.3 = bf16[24,2048]{1,0:T(8,128)(2,1)S(1)} all-gather(bf16[24,512]{1,0:T(8,128)(2,1)S(1)} %convolution_convert_fusion), channel_id=1, replica_groups=mesh['ind'=8,'snp'=4] {'snp'}, dimensions={1}, use_global_device_ids=true | all-gather | bytes 122880 | tf_op jit(solution)/shard_map/all_gather | solution.py:71
  167.6 78.2 %while.22 = (s32[]{:T(128)}, f32[24,2048]{1,0:T(8,128)S(1)}, bf16[16,24,128]{2,1,0:T(8,128)(2,1)S(1)}, s32[16,32,2048]{2,0,1:T(8,128)}, f32[2048]{0:T(1024)S(1)}, /*index=5*/f32[2048]{0:T(1024)S(1)}, s32[]{:T(128)}, s32[]{:T(128)}) while((s32[]{:T(128)}, f32[24,2048]{1,0:T(8,128)S(1)}, bf16[16,24,128]{2,1,0:T(8,128)(2,1)S(1)}, ...), condition=%wide.region_7.8_spmd.clone, body=%wide.region_6.7_spmd.clone.sunk | while | flops 16351235 | bytes 3823719 | solution.py:50
  167.6 3.3 %fusion.45 = (bf16[32,1,2048]{2,1,0:T(2,128)(2,1)S(1)}, bf16[32,1,2048]{2,1,0:T(2,128)(2,1)S(1)}, bf16[32,1,2048]{2,1,0:T(2,128)(2,1)S(1)}, bf16[32,1,2048]{2,1,0:T(2,128)(2,1)S(1)}) fusion(f32[2048]{0:T(1024)S(1)} %get-tuple-element.268, f32[2048]{0:T(1024)S(1)} %get-tuple-element.267, s32[16,32,2048]{2,0,1:T(8,128)} %get-tuple-element.266, ...), kind=kLoop, calls=%fused_computation.29.clone.1 | loop fusion | flops 1572864 | bytes 802820 | tf_op jit(solution)/shard_map/while/body/eval_jaxpr/convert_element_type | solution.py:14
  172.5 3.3 %fusion.45 = (bf16[32,1,2048]{2,1,0:T(2,128)(2,1)S(1)}, bf16[32,1,2048]{2,1,0:T(2,128)(2,1)S(1)}, bf16[32,1,2048]{2,1,0:T(2,128)(2,1)S(1)}, bf16[32,1,2048]{2,1,0:T(2,128)(2,1)S(1)}) fusion(f32[2048]{0:T(1024)S(1)} %get-tuple-element.268, f32[2048]{0:T(1024)S(1)} %get-tuple-element.267, s32[16,32,2048]{2,0,1:T(8,128)} %get-tuple-element.266, ...), kind=kLoop, calls=%fused_computation.29.clone.1 | loop fusion | flops 1572864 | bytes 802820 | tf_op jit(solution)/shard_map/while/body/eval_jaxpr/convert_element_type | solution.py:14
  177.4 3.3 %fusion.45 = (bf16[32,1,2048]{2,1,0:T(2,128)(2,1)S(1)}, bf16[32,1,2048]{2,1,0:T(2,128)(2,1)S(1)}, bf16[32,1,2048]{2,1,0:T(2,128)(2,1)S(1)}, bf16[32,1,2048]{2,1,0:T(2,128)(2,1)S(1)}) fusion(f32[2048]{0:T(1024)S(1)} %get-tuple-element.268, f32[2048]{0:T(1024)S(1)} %get-tuple-element.267, s32[16,32,2048]{2,0,1:T(8,128)} %get-tuple-element.266, ...), kind=kLoop, calls=%fused_computation.29.clone.1 | loop fusion | flops 1572864 | bytes 802820 | tf_op jit(solution)/shard_map/while/body/eval_jaxpr/convert_element_type | solution.py:14
  187.1 3.3 %fusion.45 = (bf16[32,1,2048]{2,1,0:T(2,128)(2,1)S(1)}, bf16[32,1,2048]{2,1,0:T(2,128)(2,1)S(1)}, bf16[32,1,2048]{2,1,0:T(2,128)(2,1)S(1)}, bf16[32,1,2048]{2,1,0:T(2,128)(2,1)S(1)}) fusion(f32[2048]{0:T(1024)S(1)} %get-tuple-element.268, f32[2048]{0:T(1024)S(1)} %get-tuple-element.267, s32[16,32,2048]{2,0,1:T(8,128)} %get-tuple-element.266, ...), kind=kLoop, calls=%fused_computation.29.clone.1 | loop fusion | flops 1572864 | bytes 802820 | tf_op jit(solution)/shard_map/while/body/eval_jaxpr/convert_element_type | solution.py:14
  196.9 3.3 %fusion.45 = (bf16[32,1,2048]{2,1,0:T(2,128)(2,1)S(1)}, bf16[32,1,2048]{2,1,0:T(2,128)(2,1)S(1)}, bf16[32,1,2048]{2,1,0:T(2,128)(2,1)S(1)}, bf16[32,1,2048]{2,1,0:T(2,128)(2,1)S(1)}) fusion(f32[2048]{0:T(1024)S(1)} %get-tuple-element.268, f32[2048]{0:T(1024)S(1)} %get-tuple-element.267, s32[16,32,2048]{2,0,1:T(8,128)} %get-tuple-element.266, ...), kind=kLoop, calls=%fused_computation.29.clone.1 | loop fusion | flops 1572864 | bytes 802820 | tf_op jit(solution)/shard_map/while/body/eval_jaxpr/convert_element_type | solution.py:14
  201.8 3.3 %fusion.45 = (bf16[32,1,2048]{2,1,0:T(2,128)(2,1)S(1)}, bf16[32,1,2048]{2,1,0:T(2,128)(2,1)S(1)}, bf16[32,1,2048]{2,1,0:T(2,128)(2,1)S(1)}, bf16[32,1,2048]{2,1,0:T(2,128)(2,1)S(1)}) fusion(f32[2048]{0:T(1024)S(1)} %get-tuple-element.268, f32[2048]{0:T(1024)S(1)} %get-tuple-element.267, s32[16,32,2048]{2,0,1:T(8,128)} %get-tuple-element.266, ...), kind=kLoop, calls=%fused_computation.29.clone.1 | loop fusion | flops 1572864 | bytes 802820 | tf_op jit(solution)/shard_map/while/body/eval_jaxpr/convert_element_type | solution.py:14
  211.6 3.3 %fusion.45 = (bf16[32,1,2048]{2,1,0:T(2,128)(2,1)S(1)}, bf16[32,1,2048]{2,1,0:T(2,128)(2,1)S(1)}, bf16[32,1,2048]{2,1,0:T(2,128)(2,1)S(1)}, bf16[32,1,2048]{2,1,0:T(2,128)(2,1)S(1)}) fusion(f32[2048]{0:T(1024)S(1)} %get-tuple-element.268, f32[2048]{0:T(1024)S(1)} %get-tuple-element.267, s32[16,32,2048]{2,0,1:T(8,128)} %get-tuple-element.266, ...), kind=kLoop, calls=%fused_computation.29.clone.1 | loop fusion | flops 1572864 | bytes 802820 | tf_op jit(solution)/shard_map/while/body/eval_jaxpr/convert_element_type | solution.py:14
  221.4 3.3 %fusion.45 = (bf16[32,1,2048]{2,1,0:T(2,128)(2,1)S(1)}, bf16[32,1,2048]{2,1,0:T(2,128)(2,1)S(1)}, bf16[32,1,2048]{2,1,0:T(2,128)(2,1)S(1)}, bf16[32,1,2048]{2,1,0:T(2,128)(2,1)S(1)}) fusion(f32[2048]{0:T(1024)S(1)} %get-tuple-element.268, f32[2048]{0:T(1024)S(1)} %get-tuple-element.267, s32[16,32,2048]{2,0,1:T(8,128)} %get-tuple-element.266, ...), kind=kLoop, calls=%fused_computation.29.clone.1 | loop fusion | flops 1572864 | bytes 802820 | tf_op jit(solution)/shard_map/while/body/eval_jaxpr/convert_element_type | solution.py:14
  226.2 3.3 %fusion.45 = (bf16[32,1,2048]{2,1,0:T(2,128)(2,1)S(1)}, bf16[32,1,2048]{2,1,0:T(2,128)(2,1)S(1)}, bf16[32,1,2048]{2,1,0:T(2,128)(2,1)S(1)}, bf16[32,1,2048]{2,1,0:T(2,128)(2,1)S(1)}) fusion(f32[2048]{0:T(1024)S(1)} %get-tuple-element.268, f32[2048]{0:T(1024)S(1)} %get-tuple-element.267, s32[16,32,2048]{2,0,1:T(8,128)} %get-tuple-element.266, ...), kind=kLoop, calls=%fused_computation.29.clone.1 | loop fusion | flops 1572864 | bytes 802820 | tf_op jit(solution)/shard_map/while/body/eval_jaxpr/convert_element_type | solution.py:14
  246.5 70.0 %all-reduce.2.cloned.1.call-done = bf16[24,2048]{1,0:T(8,128)(2,1)} async-done(((bf16[24,2048]{1,0:T(8,128)(2,1)}), bf16[24,2048]{1,0:T(8,128)(2,1)}) %all-reduce.2.cloned.1.call-update) | async-done | bytes 98320 | tf_op jit(solution)/shard_map/psum | solution.py:73
  (128 shorter events, 83.7 us)
Async XLA Ops:
  6.5 108.6 %reduce-scatter.2.cloned.1.call-start = ((), (), s32[]{:S(2)}) async-start(), calls=%async_computation.1 | async-start | bytes 122880 | tf_op jit(solution)/shard_map/reduce_scatter | solution.py:56
  6.5 6.6 %copy-start = (bf16[24,2048]{1,0:T(8,128)(2,1)S(1)}, bf16[24,2048]{1,0:T(8,128)(2,1)}, u32[]{:S(2)}) copy-start(bf16[24,2048]{1,0:T(8,128)(2,1)} %param.9) | copy-start | bytes 294916
  6.5 6.6 %copy-start.1 = (f32[2048]{0:T(1024)S(1)}, f32[2048]{0:T(1024)}, u32[]{:S(2)}) copy-start(f32[2048]{0:T(1024)} %param.10) | copy-start | bytes 24580
  6.5 6.6 %copy-start.2 = (f32[2048]{0:T(1024)S(1)}, f32[2048]{0:T(1024)}, u32[]{:S(2)}) copy-start(f32[2048]{0:T(1024)} %param.11) | copy-start | bytes 24580
  92.8 223.7 %all-reduce.2.cloned.1.call-start = ((), (), s32[]{:S(2)}) async-start(), calls=%async_computation.2 | async-start | bytes 196608 | tf_op jit(solution)/shard_map/psum | solution.py:73
Sparse Core Ops, SparseCore 0:
  92.9 22.2 reduce-scatter.1
  246.6 69.8 all-reduce.1
where the time goes:
time: 326 us; the launch traced here: 325 us
  other arithmetic  153 us (47%)
  waiting for transfers between devices  92.4 us (28%)
  blocking collectives  45.1 us (14%)
  between operations  13.5 us (4%)
  local copies, waits for them, and re-layouts  11.2 us (3%)
  matrix products  9.14 us (3%)
    convert_element_type x32, other arithmetic, unpack(): ((codes.astype(jnp.float32) - allele_mean) * allele_scale).astype(jnp.bfl...  106 us
    psum x1, waiting for transfers between devices, on_device(): return lax.psum(product.astype(jnp.bfloat16), 'ind').astype(jnp.float32)  70 us
    psum x1, blocking collectives, on_device(): total = lax.psum(gram, ('ind', 'snp'))  39.4 us
    another operation x32, other arithmetic, unpack(): stacked = jnp.stack(planes, axis=1)  39.1 us
    reduce_scatter x1, waiting for transfers between devices, on_device(): lax.psum_scatter(partial_sketch.astype(jnp.bfloat16), 'snp', scatter_dime...  22.3 us
    while x1, local copies, waits for them, and re-layouts, sketch_rows(): pieces = lax.map(one_block, blocks)  6.58 us
  transfers between devices with their start and end apart: 2, of which 2 were waited for; matrix products, arithmetic and copies ran while one was open for 0% of the time, Pallas kernels for 0%

commit v1 on v0

v1 whole, which is shorter than its diff:
```python
import functools

import jax
import jax.numpy as jnp
from jax import lax
from jax.experimental import pallas as pl
from jax.experimental.pallas import tpu as pltpu
from jax.sharding import PartitionSpec as P

MESH = pl.DeviceIdType.MESH
CORES = 2
CHUNKS = 4
PLANES = 4


def fold(x):
    half = x.shape[1] // 2
    return jnp.concatenate([x[:, :half], x[:, half:]], axis=0)


def unfold(x):
    rows = x.shape[0] // 2
    return jnp.concatenate([x[:rows], x[rows:]], axis=1)


def dot_nt(a, b):
    return lax.dot_general(
        a, b, (((1,), (1,)), ((), ())), preferred_element_type=jnp.float32
    )


def inverse_factor(packed, rank):
    groups = rank // 8
    a = jnp.concatenate([packed[:, 32 * g : 32 * g + 32] for g in range(groups)], axis=0)
    shape = (rank, 128)
    row_id = lax.broadcasted_iota(jnp.int32, shape, 0)
    lane_id = lax.broadcasted_iota(jnp.int32, shape, 1)
    eye = jnp.where(lane_id == row_id + 32, 1.0, 0.0).astype(jnp.float32)
    m = jnp.concatenate([a, jnp.zeros((rank, 96), jnp.float32)], axis=1) + eye
    rows1 = lax.broadcasted_iota(jnp.int32, (rank, 1), 0)
    for p in range(rank - 1):
        factor = jnp.where(rows1 > p, m[:, p : p + 1] / m[p : p + 1, p : p + 1], 0.0)
        m = m - factor * m[p : p + 1, :]
    pivots = jnp.sum(jnp.where(lane_id == row_id, m, 0.0), axis=1, keepdims=True)
    return m[:, 32 : 32 + rank] * (1.0 / jnp.sqrt(pivots))


def kernel(
    n, ny, g_hbm, probe_ref, mean_ref, scale_ref, out_ref,
    words, codes, weights, means, scales, sk, rx_core, ry, s_out, s_in, s_cat,
    rg, qacc, rs_out, rs_in, ag,
    load_sem, core_send, core_recv, y_send, y_recv, s_send, s_recv,
    g_send, g_recv, rs_send, rs_recv, ag_send, ag_recv,
):
    rank, cols = probe_ref.shape
    w = cols // n
    half = words.shape[0] // 2
    cw = half // CHUNKS
    ci = cw * PLANES
    group = n * CORES
    ind = lax.axis_index("ind")
    snp = lax.axis_index("snp")
    core = lax.rem(snp, CORES)
    y = lax.div(snp, CORES)
    other = snp + 1 - 2 * core
    gme = ind * CORES + core

    def load(c):
        h, k = divmod(c, CHUNKS) if isinstance(c, int) else (lax.div(c, CHUNKS), lax.rem(c, CHUNKS))
        where = jnp.where(h == 0, 1 - core, core)
        row = pl.multiple_of(where * half + k * cw, 8)
        at = pl.multiple_of(c * cw, 8)
        return pltpu.make_async_copy(
            g_hbm.at[pl.ds(row, cw), :], words.at[pl.ds(at, cw), :], load_sem.at[c]
        )

    for c in range(2 * CHUNKS):
        load(c).start()

    barrier = pltpu.get_barrier_semaphore()

    def greet(k, carry):
        to = lax.rem(gme + k, group)
        pl.semaphore_signal(
            barrier, inc=1, device_id=(lax.div(to, CORES), y * CORES + lax.rem(to, CORES)),
            device_id_type=MESH,
        )
        return carry

    lax.fori_loop(1, group, greet, 0)
    for k in range(1, ny):
        pl.semaphore_signal(
            barrier, inc=1, device_id=(ind, lax.rem(y + k, ny) * CORES + core),
            device_id_type=MESH,
        )

    scale = scale_ref[...]
    mean = mean_ref[...]
    scaled = probe_ref[...].astype(jnp.float32) * scale
    const = jnp.sum(scaled * mean, axis=1, keepdims=True)
    high = scaled.astype(jnp.bfloat16).astype(jnp.float32)
    both = jnp.concatenate([high, scaled - high], axis=0).astype(jnp.bfloat16)
    for b in range(n):
        weights[b] = both[:, b * w : (b + 1) * w]
        means[b] = mean[:, b * w : (b + 1) * w]
        scales[b] = scale[:, b * w : (b + 1) * w]

    def sketch_chunk(c):
        load(c).wait()
        at = pl.multiple_of(c * cw, 8)
        total = jnp.zeros((2 * rank, ci), jnp.float32)
        for b in range(n):
            packed = words[pl.ds(at, cw), b * w : (b + 1) * w]
            for k in range(PLANES):
                plane = ((packed >> (2 * k)) & 3).astype(jnp.float32).astype(jnp.bfloat16)
                codes[b, pl.ds(pl.multiple_of(c * ci + k * cw, 16), cw), :] = plane
            total += dot_nt(weights[b], codes[b, pl.ds(pl.multiple_of(c * ci, 16), ci), :])
        return total[:rank] + total[rank:] - const

    def first(c, carry):
        sk[c] = sketch_chunk(c)
        return carry

    lax.fori_loop(0, CHUNKS, first, 0)
    pl.semaphore_wait(barrier, group - 1 + ny - 1)
    core_copy = pltpu.make_async_remote_copy(
        src_ref=sk, dst_ref=rx_core, send_sem=core_send, recv_sem=core_recv,
        device_id=(ind, other), device_id_type=MESH,
    )
    core_copy.start()

    def y_copy(k, c, slot):
        return pltpu.make_async_remote_copy(
            src_ref=ry.at[y, c], dst_ref=ry.at[slot, c],
            send_sem=y_send.at[k, c], recv_sem=y_recv.at[slot, c],
            device_id=(ind, lax.rem(y + k, ny) * CORES + core), device_id_type=MESH,
        )

    def second_chunk(c):
        mine = sketch_chunk(CHUNKS + c) + rx_core[c]
        ry[y, c] = fold(mine).astype(jnp.bfloat16)
        for k in range(1, ny):
            y_copy(k, c, y).start()

    def second(c, carry):
        second_chunk(c)
        return carry

    core_copy.wait_recv()
    lax.fori_loop(0, CHUNKS, second, 0)
    core_copy.wait_send()

    pieces = []
    gram = jnp.zeros((rank, rank), jnp.float32)
    for c in range(CHUNKS):
        for k in range(1, ny):
            y_copy(k, c, lax.rem(y + k, ny)).wait_recv()
        total = ry[0, c].astype(jnp.float32)
        for k in range(1, ny):
            total += ry[k, c].astype(jnp.float32)
        rounded = total.astype(jnp.bfloat16)
        s_out[c] = rounded
        piece = unfold(rounded.astype(jnp.float32))
        pieces.append(piece)
    s_copy = pltpu.make_async_remote_copy(
        src_ref=s_out, dst_ref=s_in, send_sem=s_send, recv_sem=s_recv,
        device_id=(ind, other), device_id_type=MESH,
    )
    s_copy.start()
    mine = jnp.concatenate(pieces, axis=1)
    row_sum = jnp.sum(mine, axis=1, keepdims=True)
    mine = mine.astype(jnp.bfloat16)
    s_cat[1] = mine
    gram = dot_nt(mine, mine)
    pad = jnp.zeros((8, 32 - rank), jnp.float32)
    parts = []
    for g in range(rank // 8):
        parts += [gram[8 * g : 8 * g + 8, :], pad]
    parts.append(jnp.zeros((8, 128 - 4 * rank), jnp.float32))
    rg[gme] = jnp.concatenate(parts, axis=1)

    def g_copy(k, slot):
        to = lax.rem(gme + k, group)
        return pltpu.make_async_remote_copy(
            src_ref=rg.at[gme], dst_ref=rg.at[slot],
            send_sem=g_send.at[k], recv_sem=g_recv.at[slot],
            device_id=(lax.div(to, CORES), y * CORES + lax.rem(to, CORES)),
            device_id_type=MESH,
        )

    def g_start(k, carry):
        g_copy(k, gme).start()
        return carry

    lax.fori_loop(1, group, g_start, 0)

    span = CHUNKS * ci

    def own_half(b, carry):
        qacc[b] = jnp.dot(
            s_cat[1], codes[b, span : 2 * span, :], preferred_element_type=jnp.float32
        )
        return carry

    lax.fori_loop(0, n, own_half, 0)
    s_copy.wait_recv()
    theirs = jnp.concatenate(
        [unfold(s_in[c].astype(jnp.float32)) for c in range(CHUNKS)], axis=1
    )
    row_sum = row_sum + jnp.sum(theirs, axis=1, keepdims=True)
    s_cat[0] = theirs.astype(jnp.bfloat16)

    def rs_copy(k, slot):
        to = lax.rem(ind + k, n)
        return pltpu.make_async_remote_copy(
            src_ref=rs_out.at[to], dst_ref=rs_in.at[slot],
            send_sem=rs_send.at[k], recv_sem=rs_recv.at[slot],
            device_id=(to, snp), device_id_type=MESH,
        )

    def block(b):
        q = qacc[b] + jnp.dot(
            s_cat[0], codes[b, 0:span, :], preferred_element_type=jnp.float32
        )
        return fold(scales[b] * (q - means[b] * row_sum)).astype(jnp.bfloat16)

    def other_half(k, carry):
        b = lax.rem(ind + k, n)
        rs_out[b] = block(b)
        rs_copy(k, ind).start()
        return carry

    lax.fori_loop(1, n, other_half, 0)
    rs_in[ind] = block(ind)

    def g_wait(k, carry):
        g_copy(k, lax.rem(gme + k, group)).wait_recv()
        return carry

    lax.fori_loop(1, group, g_wait, 0)
    packed = lax.fori_loop(1, group, lambda k, t: t + rg[k], rg[0])
    lower_inv = inverse_factor(packed, rank)

    def rs_wait(k, carry):
        rs_copy(k, lax.rem(ind + k, n)).wait_recv()
        return carry

    lax.fori_loop(1, n, rs_wait, 0)
    q = lax.fori_loop(
        1, n, lambda k, t: t + rs_in[k].astype(jnp.float32), rs_in[0].astype(jnp.float32)
    )
    loadings = jnp.dot(
        lower_inv, unfold(q), precision=lax.Precision.HIGHEST,
        preferred_element_type=jnp.float32,
    )
    ag[ind] = fold(loadings).astype(jnp.bfloat16)

    def ag_copy(k, slot):
        return pltpu.make_async_remote_copy(
            src_ref=ag.at[ind], dst_ref=ag.at[slot],
            send_sem=ag_send.at[k], recv_sem=ag_recv.at[slot],
            device_id=(lax.rem(ind + k, n), snp), device_id_type=MESH,
        )

    def ag_start(k, carry):
        ag_copy(k, ind).start()
        return carry

    lax.fori_loop(1, n, ag_start, 0)

    def drain(k, carry):
        ag_copy(k, lax.rem(ind + k, n)).wait_recv()
        rs_copy(k, ind).wait_send()
        return carry

    lax.fori_loop(1, n, drain, 0)
    for b in range(n):
        out_ref[:, b * w : (b + 1) * w] = unfold(ag[b].astype(jnp.float32))

    def drain_ag(k, carry):
        ag_copy(k, ind).wait_send()
        return carry

    lax.fori_loop(1, n, drain_ag, 0)

    def drain_g(k, carry):
        g_copy(k, gme).wait_send()
        return carry

    lax.fori_loop(1, group, drain_g, 0)
    s_copy.wait_send()
    for c in range(CHUNKS):
        for k in range(1, ny):
            y_copy(k, c, y).wait_send()


def on_device(n, ny, genotype, probe, allele_mean, allele_scale):
    word_rows, cols = genotype.shape
    rank = probe.shape[0]
    w = cols // n
    ci = word_rows // (2 * CHUNKS) * PLANES
    group = n * CORES
    f32, b16 = jnp.float32, jnp.bfloat16
    dma = pltpu.SemaphoreType.DMA
    vmem = pl.BlockSpec(memory_space=pltpu.VMEM)
    return pl.pallas_call(
        functools.partial(kernel, n, ny),
        out_shape=jax.ShapeDtypeStruct((rank, cols), f32),
        in_specs=[pl.BlockSpec(memory_space=pl.ANY), vmem, vmem, vmem],
        out_specs=vmem,
        scratch_shapes=[
            pltpu.VMEM((word_rows, cols), jnp.int32),
            pltpu.VMEM((n, PLANES * word_rows, w), b16),
            pltpu.VMEM((n, 2 * rank, w), b16),
            pltpu.VMEM((n, 1, w), f32),
            pltpu.VMEM((n, 1, w), f32),
            pltpu.VMEM((CHUNKS, rank, ci), f32),
            pltpu.VMEM((CHUNKS, rank, ci), f32),
            pltpu.VMEM((ny, CHUNKS, 2 * rank, ci // 2), b16),
            pltpu.VMEM((CHUNKS, 2 * rank, ci // 2), b16),
            pltpu.VMEM((CHUNKS, 2 * rank, ci // 2), b16),
            pltpu.VMEM((2, rank, CHUNKS * ci), b16),
            pltpu.VMEM((group, 8, 128), f32),
            pltpu.VMEM((n, rank, w), f32),
            pltpu.VMEM((n, 2 * rank, w // 2), b16),
            pltpu.VMEM((n, 2 * rank, w // 2), b16),
            pltpu.VMEM((n, 2 * rank, w // 2), b16),
            dma((2 * CHUNKS,)),
            dma, dma,
            dma((ny, CHUNKS)), dma((ny, CHUNKS)),
            dma, dma,
            dma((group,)), dma((group,)),
            dma((n,)), dma((n,)),
            dma((n,)), dma((n,)),
        ],
        compiler_params=pltpu.CompilerParams(
            collective_id=0, has_side_effects=True, vmem_limit_bytes=48 * 1024 * 1024
        ),
        cost_estimate=pl.CostEstimate(
            flops=4 * rank * PLANES * word_rows * cols,
            bytes_accessed=4 * word_rows * cols,
            transcendentals=0,
        ),
    )(genotype, probe, allele_mean.reshape(1, cols), allele_scale.reshape(1, cols))


def solution(mesh):
    n = mesh.shape["ind"]
    ny = mesh.shape["snp"] // CORES
    return jax.shard_map(
        functools.partial(on_device, n, ny),
        mesh=mesh,
        in_specs=(P("ind", "snp"), P(None, "snp"), P("snp"), P("snp")),
        out_specs=P(None, "snp"),
        check_vma=False,
    )
```

time: 326 us -> 31 us (0.10)
  other arithmetic: 153 us -> 0 us
  waiting for transfers between devices: 92.4 us -> 0 us
  blocking collectives: 45.1 us -> 0 us
  Pallas kernels: 0 us -> 25.5 us
  between operations: 13.5 us -> 0.01 us
  matrix products: 9.14 us -> 0 us
  local copies, waits for them, and re-layouts: 11.2 us -> 5.15 us
    convert_element_type x34 -> x0, other arithmetic: 108 us -> none  [the longest x32 106 us: unpack(): ((codes.astype(jnp.float32) - allele_mean) * allele_scale).astype(jnp.bfl...]
    psum x1 -> x0, waiting for transfers between devices: 70 us -> none  [on_device(): return lax.psum(product.astype(jnp.bfloat16), 'ind').astype(jnp.float32)]
    another operation x37 -> x0, other arithmetic: 44.5 us -> none  [the longest x32 39.1 us: unpack(): stacked = jnp.stack(planes, axis=1)]
    psum x1 -> x0, blocking collectives: 39.4 us -> none  [on_device(): total = lax.psum(gram, ('ind', 'snp'))]
    pallas_call x0 -> x1, Pallas kernels: none -> 25.5 us  [on_device(): pl.pallas_call(functools.partial(kernel, n, ny), out_shape=jax.ShapeDtype...]
    reduce_scatter x1 -> x0, waiting for transfers between devices: 22.3 us -> none  [on_device(): lax.psum_scatter(partial_sketch.astype(jnp.bfloat16), 'snp', scatter_dime...]
    dot_general x33 -> x0, matrix products: 8.18 us -> none  [the longest x16 4.13 us: one_block(): lax.dot_general(probe, zed, (((1,), (1,)), ((), ())), preferred_element_t...]
    while x1 -> x0, local copies, waits for them, and re-layouts: 6.58 us -> none  [sketch_rows(): pieces = lax.map(one_block, blocks)]
  transfers between devices with their start and end apart: 2 -> 0, of which waited for: 2 -> 0; matrix products, arithmetic and copies ran while one was open for 0% -> 0% of each run, Pallas kernels for 0% -> 0%
where the time goes in v1:
time: 31 us; the launch traced here: 30.7 us
  Pallas kernels  25.5 us (82%)
  local copies, waits for them, and re-layouts  5.15 us (17%)
    pallas_call x1, Pallas kernels, on_device(): pl.pallas_call(functools.partial(kernel, n, ny), out_shape=jax.ShapeDtype...  25.5 us
    unnamed x9, local copies, waits for them, and re-layouts  5.15 us

profile of v1, /device:TPU:0, one launch (start us, length us, event | category | flops | bytes accessed | tf_op | source)
XLA Modules:
  0.0 30.7 jit_solution(7161344848874110531)
XLA Ops:
  0.0 0.0 copy-start
  0.0 2.2 %copy-done = s32[512,2048]{1,0:T(8,128)S(1)} copy-done((s32[512,2048]{1,0:T(8,128)S(1)}, s32[512,2048]{1,0:T(8,128)}, u32[]{:S(2)}) %copy-start) | copy-done | bytes 4194328
  2.2 0.0 copy-start.1
  2.2 0.9 %copy-done.1 = bf16[24,2048]{1,0:T(8,128)(2,1)S(1)} copy-done((bf16[24,2048]{1,0:T(8,128)(2,1)S(1)}, bf16[24,2048]{1,0:T(8,128)(2,1)}, u32[]{:S(2)}) %copy-start.1) | copy-done | bytes 98328
  3.1 0.0 copy-start.2
  3.1 0.7 %copy-done.2 = f32[2048]{0:T(1024)S(1)} copy-done((f32[2048]{0:T(1024)S(1)}, f32[2048]{0:T(1024)}, u32[]{:S(2)}) %copy-start.2) | copy-done | bytes 8216
  3.8 0.0 copy-start.3
  3.8 0.7 %copy-done.3 = f32[2048]{0:T(1024)S(1)} copy-done((f32[2048]{0:T(1024)S(1)}, f32[2048]{0:T(1024)}, u32[]{:S(2)}) %copy-start.3) | copy-done | bytes 8216
  4.5 25.5 %shard_map.46 = f32[24,2048]{1,0:T(8,128)S(1)} custom-call(s32[512,2048]{1,0:T(8,128)S(1)} %copy-done, bf16[24,2048]{1,0:T(8,128)(2,1)S(1)} %copy-done.1, f32[1,2048]{1,0:T(1,128)S(1)} %bitcast.2, f32[1,2048]{1,0:T(1,128)S(1)} %bitcast.3), custom_call_target="tpu_custom_call" | custom-call | flops 402653184 | bytes 4194304 | tf_op jit(solution)/shard_map/pallas_call | solution.py:306
  30.0 0.7 %copy.6 = f32[24,2048]{1,0:T(8,128)} copy(f32[24,2048]{1,0:T(8,128)S(1)} %shard_map.46) | data formatting | bytes 393216
Async XLA Ops:
  0.0 2.2 %copy-start = (s32[512,2048]{1,0:T(8,128)S(1)}, s32[512,2048]{1,0:T(8,128)}, u32[]{:S(2)}) copy-start(s32[512,2048]{1,0:T(8,128)} %g_hbm.1) | copy-start | bytes 12582916
  2.2 0.9 %copy-start.1 = (bf16[24,2048]{1,0:T(8,128)(2,1)S(1)}, bf16[24,2048]{1,0:T(8,128)(2,1)}, u32[]{:S(2)}) copy-start(bf16[24,2048]{1,0:T(8,128)(2,1)} %probe_ref.1) | copy-start | bytes 294916
  3.1 0.7 %copy-start.2 = (f32[2048]{0:T(1024)S(1)}, f32[2048]{0:T(1024)}, u32[]{:S(2)}) copy-start(f32[2048]{0:T(1024)} %param.6) | copy-start | bytes 24580
  3.8 0.7 %copy-start.3 = (f32[2048]{0:T(1024)S(1)}, f32[2048]{0:T(1024)}, u32[]{:S(2)}) copy-start(f32[2048]{0:T(1024)} %param.7) | copy-start | bytes 24580

commit v2 on v1

--- a/solution.py
+++ b/solution.py
@@ -46,13 +46,13 @@
 
 
 def kernel(
-    n, ny, g_hbm, probe_ref, mean_ref, scale_ref, out_ref,
-    words, codes, weights, means, scales, sk, rx_core, ry, s_out, s_in, s_cat,
+    n, ny, g_hbm, probe_hbm, mean_hbm, scale_hbm, out_ref,
+    words, probe_ref, mean_ref, scale_ref, codes, weights, means, scales, sk, rx_core, ry, s_out, s_in, s_cat, row_sums,
     rg, qacc, rs_out, rs_in, ag,
-    load_sem, core_send, core_recv, y_send, y_recv, s_send, s_recv,
+    load_sem, small_sem, core_send, core_recv, y_send, y_recv, s_send, s_recv,
     g_send, g_recv, rs_send, rs_recv, ag_send, ag_recv,
 ):
-    rank, cols = probe_ref.shape
+    rank, cols = probe_hbm.shape
     w = cols // n
     half = words.shape[0] // 2
     cw = half // CHUNKS
@@ -74,6 +74,13 @@
             g_hbm.at[pl.ds(row, cw), :], words.at[pl.ds(at, cw), :], load_sem.at[c]
         )
 
+    small = [
+        pltpu.make_async_copy(probe_hbm, probe_ref, small_sem.at[0]),
+        pltpu.make_async_copy(mean_hbm, mean_ref, small_sem.at[1]),
+        pltpu.make_async_copy(scale_hbm, scale_ref, small_sem.at[2]),
+    ]
+    for copy in small:
+        copy.start()
     for c in range(2 * CHUNKS):
         load(c).start()
 
@@ -94,6 +101,9 @@
             device_id_type=MESH,
         )
 
+    qacc[...] = jnp.zeros_like(qacc)
+    for copy in small:
+        copy.wait()
     scale = scale_ref[...]
     mean = mean_ref[...]
     scaled = probe_ref[...].astype(jnp.float32) * scale
@@ -111,24 +121,17 @@
         total = jnp.zeros((2 * rank, ci), jnp.float32)
         for b in range(n):
             packed = words[pl.ds(at, cw), b * w : (b + 1) * w]
-            for k in range(PLANES):
-                plane = ((packed >> (2 * k)) & 3).astype(jnp.float32).astype(jnp.bfloat16)
-                codes[b, pl.ds(pl.multiple_of(c * ci + k * cw, 16), cw), :] = plane
-            total += dot_nt(weights[b], codes[b, pl.ds(pl.multiple_of(c * ci, 16), ci), :])
+            tile = jnp.concatenate(
+                [((packed >> (2 * k)) & 3).astype(jnp.float32) for k in range(PLANES)], axis=0
+            ).astype(jnp.bfloat16)
+            codes[b, pl.ds(pl.multiple_of(c * ci, 16), ci), :] = tile
+            total += dot_nt(weights[b], tile)
         return total[:rank] + total[rank:] - const
 
-    def first(c, carry):
-        sk[c] = sketch_chunk(c)
-        return carry
-
-    lax.fori_loop(0, CHUNKS, first, 0)
-    pl.semaphore_wait(barrier, group - 1 + ny - 1)
     core_copy = pltpu.make_async_remote_copy(
-        src_ref=sk, dst_ref=rx_core, send_sem=core_send, recv_sem=core_recv,
+        src_ref=sk.at[0:CHUNKS], dst_ref=rx_core, send_sem=core_send, recv_sem=core_recv,
         device_id=(ind, other), device_id_type=MESH,
     )
-    core_copy.start()
-
     def y_copy(k, c, slot):
         return pltpu.make_async_remote_copy(
             src_ref=ry.at[y, c], dst_ref=ry.at[slot, c],
@@ -136,18 +139,28 @@
             device_id=(ind, lax.rem(y + k, ny) * CORES + core), device_id_type=MESH,
         )
 
-    def second_chunk(c):
-        mine = sketch_chunk(CHUNKS + c) + rx_core[c]
-        ry[y, c] = fold(mine).astype(jnp.bfloat16)
-        for k in range(1, ny):
-            y_copy(k, c, y).start()
-
-    def second(c, carry):
-        second_chunk(c)
-        return carry
-
-    core_copy.wait_recv()
-    lax.fori_loop(0, CHUNKS, second, 0)
+    def chunk(c, carry):
+        sk[c] = sketch_chunk(c)
+
+        @pl.when(c == CHUNKS - 1)
+        def _():
+            pl.semaphore_wait(barrier, group - 1 + ny - 1)
+            core_copy.start()
+
+        @pl.when(c == CHUNKS)
+        def _():
+            core_copy.wait_recv()
+
+        @pl.when(c >= CHUNKS)
+        def _():
+            j = c - CHUNKS
+            ry[y, j] = fold(sk[c] + rx_core[j]).astype(jnp.bfloat16)
+            for k in range(1, ny):
+                y_copy(k, j, y).start()
+
+        return carry
+
+    lax.fori_loop(0, 2 * CHUNKS, chunk, 0)
     core_copy.wait_send()
 
     pieces = []
@@ -168,7 +181,7 @@
     )
     s_copy.start()
     mine = jnp.concatenate(pieces, axis=1)
-    row_sum = jnp.sum(mine, axis=1, keepdims=True)
+    row_sums[...] = jnp.broadcast_to(jnp.sum(mine, axis=1, keepdims=True), (rank, 128))
     mine = mine.astype(jnp.bfloat16)
     s_cat[1] = mine
     gram = dot_nt(mine, mine)
@@ -196,20 +209,6 @@
 
     span = CHUNKS * ci
 
-    def own_half(b, carry):
-        qacc[b] = jnp.dot(
-            s_cat[1], codes[b, span : 2 * span, :], preferred_element_type=jnp.float32
-        )
-        return carry
-
-    lax.fori_loop(0, n, own_half, 0)
-    s_copy.wait_recv()
-    theirs = jnp.concatenate(
-        [unfold(s_in[c].astype(jnp.float32)) for c in range(CHUNKS)], axis=1
-    )
-    row_sum = row_sum + jnp.sum(theirs, axis=1, keepdims=True)
-    s_cat[0] = theirs.astype(jnp.bfloat16)
-
     def rs_copy(k, slot):
         to = lax.rem(ind + k, n)
         return pltpu.make_async_remote_copy(
@@ -218,20 +217,42 @@
             device_id=(to, snp), device_id_type=MESH,
         )
 
-    def block(b):
+    def product(t, carry):
+        later = t > n
+        h = jnp.where(later, 0, 1)
+        k = jnp.where(later, t - n, t)
+        b = lax.rem(ind + k, n)
+
+        @pl.when(t == n + 1)
+        def _():
+            s_copy.wait_recv()
+            theirs = jnp.concatenate(
+                [unfold(s_in[c].astype(jnp.float32)) for c in range(CHUNKS)], axis=1
+            )
+            row_sums[...] += jnp.broadcast_to(
+                jnp.sum(theirs, axis=1, keepdims=True), (rank, 128)
+            )
+            s_cat[0] = theirs.astype(jnp.bfloat16)
+
+        at = pl.multiple_of(h * span, 16)
         q = qacc[b] + jnp.dot(
-            s_cat[0], codes[b, 0:span, :], preferred_element_type=jnp.float32
-        )
-        return fold(scales[b] * (q - means[b] * row_sum)).astype(jnp.bfloat16)
-
-    def other_half(k, carry):
-        b = lax.rem(ind + k, n)
-        rs_out[b] = block(b)
-        rs_copy(k, ind).start()
-        return carry
-
-    lax.fori_loop(1, n, other_half, 0)
-    rs_in[ind] = block(ind)
+            s_cat[h], codes[b, pl.ds(at, span), :], preferred_element_type=jnp.float32
+        )
+        qacc[b] = q
+
+        @pl.when(later)
+        def _():
+            centred = scales[b] * (qacc[b] - means[b] * row_sums[:, 0:1])
+            rs_out[b] = fold(centred).astype(jnp.bfloat16)
+
+        @pl.when(jnp.logical_and(later, k < n))
+        def _():
+            rs_copy(k, ind).start()
+
+        return carry
+
+    lax.fori_loop(1, 2 * n + 1, product, 0)
+    rs_in[ind] = rs_out[ind]
 
     def g_wait(k, carry):
         g_copy(k, lax.rem(gme + k, group)).wait_recv()
@@ -306,26 +327,31 @@
     return pl.pallas_call(
         functools.partial(kernel, n, ny),
         out_shape=jax.ShapeDtypeStruct((rank, cols), f32),
-        in_specs=[pl.BlockSpec(memory_space=pl.ANY), vmem, vmem, vmem],
+        in_specs=[pl.BlockSpec(memory_space=pltpu.HBM)] * 4,
         out_specs=vmem,
         scratch_shapes=[
             pltpu.VMEM((word_rows, cols), jnp.int32),
+            pltpu.VMEM((rank, cols), b16),
+            pltpu.VMEM((1, cols), f32),
+            pltpu.VMEM((1, cols), f32),
             pltpu.VMEM((n, PLANES * word_rows, w), b16),
             pltpu.VMEM((n, 2 * rank, w), b16),
             pltpu.VMEM((n, 1, w), f32),
             pltpu.VMEM((n, 1, w), f32),
-            pltpu.VMEM((CHUNKS, rank, ci), f32),
+            pltpu.VMEM((2 * CHUNKS, rank, ci), f32),
             pltpu.VMEM((CHUNKS, rank, ci), f32),
             pltpu.VMEM((ny, CHUNKS, 2 * rank, ci // 2), b16),
             pltpu.VMEM((CHUNKS, 2 * rank, ci // 2), b16),
             pltpu.VMEM((CHUNKS, 2 * rank, ci // 2), b16),
             pltpu.VMEM((2, rank, CHUNKS * ci), b16),
+            pltpu.VMEM((rank, 128), f32),
             pltpu.VMEM((group, 8, 128), f32),
             pltpu.VMEM((n, rank, w), f32),
             pltpu.VMEM((n, 2 * rank, w // 2), b16),
             pltpu.VMEM((n, 2 * rank, w // 2), b16),
             pltpu.VMEM((n, 2 * rank, w // 2), b16),
             dma((2 * CHUNKS,)),
+            dma((3,)),
             dma, dma,
             dma((ny, CHUNKS)), dma((ny, CHUNKS)),
             dma, dma,
@@ -334,7 +360,7 @@
             dma((n,)), dma((n,)),
         ],
         compiler_params=pltpu.CompilerParams(
-            collective_id=0, has_side_effects=True, vmem_limit_bytes=48 * 1024 * 1024
+            collective_id=0, has_side_effects=True, vmem_limit_bytes=63 * 1024 * 1024
         ),
         cost_estimate=pl.CostEstimate(
             flops=4 * rank * PLANES * word_rows * cols,

time: 31 us -> 27 us (0.87)
  local copies, waits for them, and re-layouts: 5.15 us -> 1.62 us
    unnamed x9 -> x1, local copies, waits for them, and re-layouts: 5.15 us -> 1.62 us
where the time goes in v2:
time: 27 us; the launch traced here: 26.9 us
  Pallas kernels  25.3 us (94%)
  local copies, waits for them, and re-layouts  1.62 us (6%)
    pallas_call x1, Pallas kernels, on_device(): pl.pallas_call(functools.partial(kernel, n, ny), out_shape=jax.ShapeDtype...  25.3 us
    unnamed x1, local copies, waits for them, and re-layouts  1.62 us

profile of v2, /device:TPU:0, one launch (start us, length us, event | category | flops | bytes accessed | tf_op | source)
XLA Modules:
  0.0 26.9 jit_solution(2203111313593720586)
XLA Ops:
  0.0 25.3 %shard_map.46 = f32[24,2048]{1,0:T(8,128)} custom-call(s32[512,2048]{1,0:T(8,128)} %g_hbm.1, bf16[24,2048]{1,0:T(8,128)(2,1)} %probe_hbm.1, f32[1,2048]{1,0:T(1,128)} %bitcast.2, f32[1,2048]{1,0:T(1,128)} %bitcast.3), custom_call_target="tpu_custom_call" | custom-call | flops 402653184 | bytes 4194304 | tf_op jit(solution)/shard_map/pallas_call | solution.py:327
  25.3 1.6 %copy.6 = f32[24,2048]{1,0:T(8,128)} copy(f32[24,2048]{1,0:T(8,128)} %shard_map.46) | data formatting | bytes 393216

commit v3 on v2

--- a/solution.py
+++ b/solution.py
@@ -47,7 +47,7 @@
 
 def kernel(
     n, ny, g_hbm, probe_hbm, mean_hbm, scale_hbm, out_ref,
-    words, probe_ref, mean_ref, scale_ref, codes, weights, means, scales, sk, rx_core, ry, s_out, s_in, s_cat, row_sums,
+    words, probe_ref, mean_ref, scale_ref, codes, weights, means, scales, sk, rx_core, ry, s_out, s_in, s_cat,
     rg, qacc, rs_out, rs_in, ag,
     load_sem, small_sem, core_send, core_recv, y_send, y_recv, s_send, s_recv,
     g_send, g_recv, rs_send, rs_recv, ag_send, ag_recv,
@@ -109,23 +109,24 @@
     scaled = probe_ref[...].astype(jnp.float32) * scale
     const = jnp.sum(scaled * mean, axis=1, keepdims=True)
     high = scaled.astype(jnp.bfloat16).astype(jnp.float32)
-    both = jnp.concatenate([high, scaled - high], axis=0).astype(jnp.bfloat16)
+    both = jnp.concatenate([high, scaled - high], axis=0).T.astype(jnp.bfloat16)
     for b in range(n):
-        weights[b] = both[:, b * w : (b + 1) * w]
+        weights[b] = both[b * w : (b + 1) * w, :]
         means[b] = mean[:, b * w : (b + 1) * w]
         scales[b] = scale[:, b * w : (b + 1) * w]
 
     def sketch_chunk(c):
         load(c).wait()
         at = pl.multiple_of(c * cw, 8)
-        total = jnp.zeros((2 * rank, ci), jnp.float32)
+        total = jnp.zeros((ci, 2 * rank), jnp.float32)
         for b in range(n):
             packed = words[pl.ds(at, cw), b * w : (b + 1) * w]
             tile = jnp.concatenate(
                 [((packed >> (2 * k)) & 3).astype(jnp.float32) for k in range(PLANES)], axis=0
             ).astype(jnp.bfloat16)
             codes[b, pl.ds(pl.multiple_of(c * ci, 16), ci), :] = tile
-            total += dot_nt(weights[b], tile)
+            total += jnp.dot(tile, weights[b], preferred_element_type=jnp.float32)
+        total = total.T
         return total[:rank] + total[rank:] - const
 
     core_copy = pltpu.make_async_remote_copy(
@@ -163,9 +164,29 @@
     lax.fori_loop(0, 2 * CHUNKS, chunk, 0)
     core_copy.wait_send()
 
-    pieces = []
-    gram = jnp.zeros((rank, rank), jnp.float32)
-    for c in range(CHUNKS):
+    def s_copy(c):
+        return pltpu.make_async_remote_copy(
+            src_ref=s_out.at[c], dst_ref=s_in.at[c], send_sem=s_send.at[c], recv_sem=s_recv.at[c],
+            device_id=(ind, other), device_id_type=MESH,
+        )
+
+    def g_copy(k, slot):
+        to = lax.rem(gme + k, group)
+        return pltpu.make_async_remote_copy(
+            src_ref=rg.at[gme], dst_ref=rg.at[slot],
+            send_sem=g_send.at[k], recv_sem=g_recv.at[slot],
+            device_id=(lax.div(to, CORES), y * CORES + lax.rem(to, CORES)),
+            device_id_type=MESH,
+        )
+
+    def g_start(k, carry):
+        g_copy(k, gme).start()
+        return carry
+
+    span = CHUNKS * ci
+
+    def own_half(c, carry):
+        gram, row_sum = carry
         for k in range(1, ny):
             y_copy(k, c, lax.rem(y + k, ny)).wait_recv()
         total = ry[0, c].astype(jnp.float32)
@@ -173,41 +194,40 @@
             total += ry[k, c].astype(jnp.float32)
         rounded = total.astype(jnp.bfloat16)
         s_out[c] = rounded
+        s_copy(c).start()
         piece = unfold(rounded.astype(jnp.float32))
-        pieces.append(piece)
-    s_copy = pltpu.make_async_remote_copy(
-        src_ref=s_out, dst_ref=s_in, send_sem=s_send, recv_sem=s_recv,
-        device_id=(ind, other), device_id_type=MESH,
-    )
-    s_copy.start()
-    mine = jnp.concatenate(pieces, axis=1)
-    row_sums[...] = jnp.broadcast_to(jnp.sum(mine, axis=1, keepdims=True), (rank, 128))
-    mine = mine.astype(jnp.bfloat16)
-    s_cat[1] = mine
-    gram = dot_nt(mine, mine)
-    pad = jnp.zeros((8, 32 - rank), jnp.float32)
-    parts = []
-    for g in range(rank // 8):
-        parts += [gram[8 * g : 8 * g + 8, :], pad]
-    parts.append(jnp.zeros((8, 128 - 4 * rank), jnp.float32))
-    rg[gme] = jnp.concatenate(parts, axis=1)
-
-    def g_copy(k, slot):
-        to = lax.rem(gme + k, group)
-        return pltpu.make_async_remote_copy(
-            src_ref=rg.at[gme], dst_ref=rg.at[slot],
-            send_sem=g_send.at[k], recv_sem=g_recv.at[slot],
-            device_id=(lax.div(to, CORES), y * CORES + lax.rem(to, CORES)),
-            device_id_type=MESH,
-        )
-
-    def g_start(k, carry):
-        g_copy(k, gme).start()
-        return carry
-
-    lax.fori_loop(1, group, g_start, 0)
-
-    span = CHUNKS * ci
+        row_sum = row_sum + jnp.sum(piece, axis=1, keepdims=True)
+        piece = piece.astype(jnp.bfloat16)
+        gram = gram + dot_nt(piece, piece)
+
+        @pl.when(c == CHUNKS - 1)
+        def _():
+            pad = jnp.zeros((8, 32 - rank), jnp.float32)
+            parts = []
+            for g in range(rank // 8):
+                parts += [gram[8 * g : 8 * g + 8, :], pad]
+            parts.append(jnp.zeros((8, 128 - 4 * rank), jnp.float32))
+            rg[gme] = jnp.concatenate(parts, axis=1)
+            lax.fori_loop(1, group, g_start, 0)
+
+        at = pl.multiple_of(span + c * ci, 16)
+        for b in range(n):
+            qacc[b] += jnp.dot(
+                piece, codes[b, pl.ds(at, ci), :], preferred_element_type=jnp.float32
+            )
+        return gram, row_sum
+
+    ignored, row_sum = lax.fori_loop(
+        0, CHUNKS, own_half,
+        (jnp.zeros((rank, rank), jnp.float32), jnp.zeros((rank, 1), jnp.float32)),
+    )
+    theirs = []
+    for c in range(CHUNKS):
+        s_copy(c).wait_recv()
+        theirs.append(unfold(s_in[c].astype(jnp.float32)))
+    theirs = jnp.concatenate(theirs, axis=1)
+    row_sum = row_sum + jnp.sum(theirs, axis=1, keepdims=True)
+    s_cat[...] = theirs.astype(jnp.bfloat16)
 
     def rs_copy(k, slot):
         to = lax.rem(ind + k, n)
@@ -217,41 +237,20 @@
             device_id=(to, snp), device_id_type=MESH,
         )
 
-    def product(t, carry):
-        later = t > n
-        h = jnp.where(later, 0, 1)
-        k = jnp.where(later, t - n, t)
+    def product(k, carry):
         b = lax.rem(ind + k, n)
-
-        @pl.when(t == n + 1)
-        def _():
-            s_copy.wait_recv()
-            theirs = jnp.concatenate(
-                [unfold(s_in[c].astype(jnp.float32)) for c in range(CHUNKS)], axis=1
-            )
-            row_sums[...] += jnp.broadcast_to(
-                jnp.sum(theirs, axis=1, keepdims=True), (rank, 128)
-            )
-            s_cat[0] = theirs.astype(jnp.bfloat16)
-
-        at = pl.multiple_of(h * span, 16)
         q = qacc[b] + jnp.dot(
-            s_cat[h], codes[b, pl.ds(at, span), :], preferred_element_type=jnp.float32
-        )
-        qacc[b] = q
-
-        @pl.when(later)
-        def _():
-            centred = scales[b] * (qacc[b] - means[b] * row_sums[:, 0:1])
-            rs_out[b] = fold(centred).astype(jnp.bfloat16)
-
-        @pl.when(jnp.logical_and(later, k < n))
+            s_cat[...], codes[b, 0:span, :], preferred_element_type=jnp.float32
+        )
+        rs_out[b] = fold(scales[b] * (q - means[b] * row_sum)).astype(jnp.bfloat16)
+
+        @pl.when(k < n)
         def _():
             rs_copy(k, ind).start()
 
         return carry
 
-    lax.fori_loop(1, 2 * n + 1, product, 0)
+    lax.fori_loop(1, n + 1, product, 0)
     rs_in[ind] = rs_out[ind]
 
     def g_wait(k, carry):
@@ -296,7 +295,7 @@
 
     lax.fori_loop(1, n, drain, 0)
     for b in range(n):
-        out_ref[:, b * w : (b + 1) * w] = unfold(ag[b].astype(jnp.float32))
+        out_ref[:, b * w : (b + 1) * w] = unfold(ag[b].astype(jnp.float32)).astype(jnp.bfloat16)
 
     def drain_ag(k, carry):
         ag_copy(k, ind).wait_send()
@@ -309,8 +308,8 @@
         return carry
 
     lax.fori_loop(1, group, drain_g, 0)
-    s_copy.wait_send()
     for c in range(CHUNKS):
+        s_copy(c).wait_send()
         for k in range(1, ny):
             y_copy(k, c, y).wait_send()
 
@@ -326,7 +325,7 @@
     vmem = pl.BlockSpec(memory_space=pltpu.VMEM)
     return pl.pallas_call(
         functools.partial(kernel, n, ny),
-        out_shape=jax.ShapeDtypeStruct((rank, cols), f32),
+        out_shape=jax.ShapeDtypeStruct((rank, cols), b16),
         in_specs=[pl.BlockSpec(memory_space=pltpu.HBM)] * 4,
         out_specs=vmem,
         scratch_shapes=[
@@ -335,7 +334,7 @@
             pltpu.VMEM((1, cols), f32),
             pltpu.VMEM((1, cols), f32),
             pltpu.VMEM((n, PLANES * word_rows, w), b16),
-            pltpu.VMEM((n, 2 * rank, w), b16),
+            pltpu.VMEM((n, w, 2 * rank), b16),
             pltpu.VMEM((n, 1, w), f32),
             pltpu.VMEM((n, 1, w), f32),
             pltpu.VMEM((2 * CHUNKS, rank, ci), f32),
@@ -343,8 +342,7 @@
             pltpu.VMEM((ny, CHUNKS, 2 * rank, ci // 2), b16),
             pltpu.VMEM((CHUNKS, 2 * rank, ci // 2), b16),
             pltpu.VMEM((CHUNKS, 2 * rank, ci // 2), b16),
-            pltpu.VMEM((2, rank, CHUNKS * ci), b16),
-            pltpu.VMEM((rank, 128), f32),
+            pltpu.VMEM((rank, CHUNKS * ci), b16),
             pltpu.VMEM((group, 8, 128), f32),
             pltpu.VMEM((n, rank, w), f32),
             pltpu.VMEM((n, 2 * rank, w // 2), b16),
@@ -354,7 +352,7 @@
             dma((3,)),
             dma, dma,
             dma((ny, CHUNKS)), dma((ny, CHUNKS)),
-            dma, dma,
+            dma((CHUNKS,)), dma((CHUNKS,)),
             dma((group,)), dma((group,)),
             dma((n,)), dma((n,)),
             dma((n,)), dma((n,)),
@@ -367,7 +365,7 @@
             bytes_accessed=4 * word_rows * cols,
             transcendentals=0,
         ),
-    )(genotype, probe, allele_mean.reshape(1, cols), allele_scale.reshape(1, cols))
+    )(genotype, probe, allele_mean.reshape(1, cols), allele_scale.reshape(1, cols)).astype(f32)
 
 
 def solution(mesh):

time: 27 us -> 26.7 us (0.989)
  local copies, waits for them, and re-layouts: 1.62 us -> 0 us
  other arithmetic: 0 us -> 1.58 us
  Pallas kernels: 25.3 us -> 25 us
    unnamed x1 -> x0, local copies, waits for them, and re-layouts: 1.62 us -> none
    convert_element_type x0 -> x1, other arithmetic: none -> 1.58 us  [on_device(): return pl.pallas_call(functools.partial(kernel, n, ny), out_shape=jax.Sha...]
    pallas_call x1, Pallas kernels: 25.3 us -> 25 us  [on_device(): pl.pallas_call(functools.partial(kernel, n, ny), out_shape=jax.ShapeDtype...]
where the time goes in v3:
time: 26.7 us; the launch traced here: 26.6 us
  Pallas kernels  25 us (94%)
  other arithmetic  1.58 us (6%)
    pallas_call x1, Pallas kernels, on_device(): pl.pallas_call(functools.partial(kernel, n, ny), out_shape=jax.ShapeDtype...  25 us
    convert_element_type x1, other arithmetic, on_device(): return pl.pallas_call(functools.partial(kernel, n, ny), out_shape=jax.Sha...  1.58 us

profile of v3, /device:TPU:0, one launch (start us, length us, event | category | flops | bytes accessed | tf_op | source)
XLA Modules:
  0.0 26.6 jit_solution(7187786756933610586)
XLA Ops:
  0.0 25.0 %shard_map.46 = bf16[24,2048]{1,0:T(8,128)(2,1)} custom-call(s32[512,2048]{1,0:T(8,128)} %g_hbm.1, bf16[24,2048]{1,0:T(8,128)(2,1)} %probe_hbm.1, f32[1,2048]{1,0:T(1,128)} %bitcast.2, f32[1,2048]{1,0:T(1,128)} %bitcast.3), custom_call_target="tpu_custom_call" | custom-call | flops 402653184 | bytes 4194304 | tf_op jit(solution)/shard_map/pallas_call | solution.py:326
  25.0 1.6 %convert_element_type.3 = f32[24,2048]{1,0:T(8,128)} convert(bf16[24,2048]{1,0:T(8,128)(2,1)} %shard_map.46) | non-fusion elementwise | flops 49152 | bytes 294912 | tf_op jit(solution)/shard_map/convert_element_type | solution.py:368

commit v4 on v3

--- a/solution.py
+++ b/solution.py
@@ -11,6 +11,7 @@
 CORES = 2
 CHUNKS = 4
 PLANES = 4
+SUBS = 2
 
 
 def fold(x):
@@ -37,10 +38,15 @@
     lane_id = lax.broadcasted_iota(jnp.int32, shape, 1)
     eye = jnp.where(lane_id == row_id + 32, 1.0, 0.0).astype(jnp.float32)
     m = jnp.concatenate([a, jnp.zeros((rank, 96), jnp.float32)], axis=1) + eye
-    rows1 = lax.broadcasted_iota(jnp.int32, (rank, 1), 0)
-    for p in range(rank - 1):
-        factor = jnp.where(rows1 > p, m[:, p : p + 1] / m[p : p + 1, p : p + 1], 0.0)
-        m = m - factor * m[p : p + 1, :]
+    for start in range(0, rank, 8):
+        spread = [jnp.broadcast_to(m[:, p : p + 1], shape) for p in range(start, start + 8)]
+        for j in range(8):
+            p = start + j
+            column = spread[j]
+            factor = jnp.where(row_id > p, column * (1.0 / column[p : p + 1, :]), 0.0)
+            m = m - factor * m[p : p + 1, :]
+            for l in range(j + 1, 8):
+                spread[l] = spread[l] - factor * spread[l][p : p + 1, :]
     pivots = jnp.sum(jnp.where(lane_id == row_id, m, 0.0), axis=1, keepdims=True)
     return m[:, 32 : 32 + rank] * (1.0 / jnp.sqrt(pivots))
 
@@ -57,13 +63,13 @@
     half = words.shape[0] // 2
     cw = half // CHUNKS
     ci = cw * PLANES
-    group = n * CORES
+    sw = cw // SUBS
+    si = ci // SUBS
     ind = lax.axis_index("ind")
     snp = lax.axis_index("snp")
     core = lax.rem(snp, CORES)
     y = lax.div(snp, CORES)
     other = snp + 1 - 2 * core
-    gme = ind * CORES + core
 
     def load(c):
         h, k = divmod(c, CHUNKS) if isinstance(c, int) else (lax.div(c, CHUNKS), lax.rem(c, CHUNKS))
@@ -87,14 +93,13 @@
     barrier = pltpu.get_barrier_semaphore()
 
     def greet(k, carry):
-        to = lax.rem(gme + k, group)
         pl.semaphore_signal(
-            barrier, inc=1, device_id=(lax.div(to, CORES), y * CORES + lax.rem(to, CORES)),
-            device_id_type=MESH,
-        )
-        return carry
-
-    lax.fori_loop(1, group, greet, 0)
+            barrier, inc=1, device_id=(lax.rem(ind + k, n), snp), device_id_type=MESH
+        )
+        return carry
+
+    lax.fori_loop(1, n, greet, 0)
+    pl.semaphore_signal(barrier, inc=1, device_id=(ind, other), device_id_type=MESH)
     for k in range(1, ny):
         pl.semaphore_signal(
             barrier, inc=1, device_id=(ind, lax.rem(y + k, ny) * CORES + core),
@@ -115,19 +120,32 @@
         means[b] = mean[:, b * w : (b + 1) * w]
         scales[b] = scale[:, b * w : (b + 1) * w]
 
+    lane = lax.broadcasted_iota(jnp.int32, (1, ci), 1)
+    plane = lax.rem(lane, si) // sw
+    plane_scale = jnp.where(
+        plane < 2, jnp.where(plane == 0, 1.0, 1 / 4), jnp.where(plane == 2, 1 / 16, 1 / 64)
+    ).astype(jnp.float32)
+
     def sketch_chunk(c):
         load(c).wait()
         at = pl.multiple_of(c * cw, 8)
-        total = jnp.zeros((ci, 2 * rank), jnp.float32)
-        for b in range(n):
-            packed = words[pl.ds(at, cw), b * w : (b + 1) * w]
-            tile = jnp.concatenate(
-                [((packed >> (2 * k)) & 3).astype(jnp.float32) for k in range(PLANES)], axis=0
-            ).astype(jnp.bfloat16)
-            codes[b, pl.ds(pl.multiple_of(c * ci, 16), ci), :] = tile
-            total += jnp.dot(tile, weights[b], preferred_element_type=jnp.float32)
-        total = total.T
-        return total[:rank] + total[rank:] - const
+        pieces = []
+        for sub in range(SUBS):
+            total = jnp.zeros((si, 2 * rank), jnp.float32)
+            for b in range(n):
+                packed = words[pl.ds(at + sub * sw, sw), b * w : (b + 1) * w]
+                tile = jnp.concatenate(
+                    [
+                        (packed & (3 << (2 * k))).astype(jnp.float32).astype(jnp.bfloat16)
+                        for k in range(PLANES)
+                    ],
+                    axis=0,
+                )
+                codes[b, pl.ds(pl.multiple_of(c * ci + sub * si, 16), si), :] = tile
+                total += jnp.dot(tile, weights[b], preferred_element_type=jnp.float32)
+            pieces.append(total.T)
+        total = jnp.concatenate(pieces, axis=1)
+        return (total[:rank] + total[rank:]) * plane_scale - const
 
     core_copy = pltpu.make_async_remote_copy(
         src_ref=sk.at[0:CHUNKS], dst_ref=rx_core, send_sem=core_send, recv_sem=core_recv,
@@ -145,7 +163,7 @@
 
         @pl.when(c == CHUNKS - 1)
         def _():
-            pl.semaphore_wait(barrier, group - 1 + ny - 1)
+            pl.semaphore_wait(barrier, n - 1 + 1 + ny - 1)
             core_copy.start()
 
         @pl.when(c == CHUNKS)
@@ -162,7 +180,6 @@
         return carry
 
     lax.fori_loop(0, 2 * CHUNKS, chunk, 0)
-    core_copy.wait_send()
 
     def s_copy(c):
         return pltpu.make_async_remote_copy(
@@ -171,16 +188,14 @@
         )
 
     def g_copy(k, slot):
-        to = lax.rem(gme + k, group)
-        return pltpu.make_async_remote_copy(
-            src_ref=rg.at[gme], dst_ref=rg.at[slot],
+        return pltpu.make_async_remote_copy(
+            src_ref=rg.at[ind], dst_ref=rg.at[slot],
             send_sem=g_send.at[k], recv_sem=g_recv.at[slot],
-            device_id=(lax.div(to, CORES), y * CORES + lax.rem(to, CORES)),
-            device_id_type=MESH,
+            device_id=(lax.rem(ind + k, n), snp), device_id_type=MESH,
         )
 
     def g_start(k, carry):
-        g_copy(k, gme).start()
+        g_copy(k, ind).start()
         return carry
 
     span = CHUNKS * ci
@@ -197,19 +212,9 @@
         s_copy(c).start()
         piece = unfold(rounded.astype(jnp.float32))
         row_sum = row_sum + jnp.sum(piece, axis=1, keepdims=True)
-        piece = piece.astype(jnp.bfloat16)
-        gram = gram + dot_nt(piece, piece)
-
-        @pl.when(c == CHUNKS - 1)
-        def _():
-            pad = jnp.zeros((8, 32 - rank), jnp.float32)
-            parts = []
-            for g in range(rank // 8):
-                parts += [gram[8 * g : 8 * g + 8, :], pad]
-            parts.append(jnp.zeros((8, 128 - 4 * rank), jnp.float32))
-            rg[gme] = jnp.concatenate(parts, axis=1)
-            lax.fori_loop(1, group, g_start, 0)
-
+        exact = piece.astype(jnp.bfloat16)
+        gram = gram + dot_nt(exact, exact)
+        piece = (piece * plane_scale).astype(jnp.bfloat16)
         at = pl.multiple_of(span + c * ci, 16)
         for b in range(n):
             qacc[b] += jnp.dot(
@@ -217,7 +222,7 @@
             )
         return gram, row_sum
 
-    ignored, row_sum = lax.fori_loop(
+    gram, row_sum = lax.fori_loop(
         0, CHUNKS, own_half,
         (jnp.zeros((rank, rank), jnp.float32), jnp.zeros((rank, 1), jnp.float32)),
     )
@@ -227,7 +232,16 @@
         theirs.append(unfold(s_in[c].astype(jnp.float32)))
     theirs = jnp.concatenate(theirs, axis=1)
     row_sum = row_sum + jnp.sum(theirs, axis=1, keepdims=True)
-    s_cat[...] = theirs.astype(jnp.bfloat16)
+    exact = theirs.astype(jnp.bfloat16)
+    gram = gram + dot_nt(exact, exact)
+    pad = jnp.zeros((8, 32 - rank), jnp.float32)
+    parts = []
+    for g in range(rank // 8):
+        parts += [gram[8 * g : 8 * g + 8, :], pad]
+    parts.append(jnp.zeros((8, 128 - 4 * rank), jnp.float32))
+    rg[ind] = jnp.concatenate(parts, axis=1)
+    lax.fori_loop(1, n, g_start, 0)
+    s_cat[...] = (theirs * jnp.concatenate([plane_scale] * CHUNKS, axis=1)).astype(jnp.bfloat16)
 
     def rs_copy(k, slot):
         to = lax.rem(ind + k, n)
@@ -254,11 +268,11 @@
     rs_in[ind] = rs_out[ind]
 
     def g_wait(k, carry):
-        g_copy(k, lax.rem(gme + k, group)).wait_recv()
-        return carry
-
-    lax.fori_loop(1, group, g_wait, 0)
-    packed = lax.fori_loop(1, group, lambda k, t: t + rg[k], rg[0])
+        g_copy(k, lax.rem(ind + k, n)).wait_recv()
+        return carry
+
+    lax.fori_loop(1, n, g_wait, 0)
+    packed = lax.fori_loop(1, n, lambda k, t: t + rg[k], rg[0])
     lower_inv = inverse_factor(packed, rank)
 
     def rs_wait(k, carry):
@@ -289,29 +303,30 @@
     lax.fori_loop(1, n, ag_start, 0)
 
     def drain(k, carry):
-        ag_copy(k, lax.rem(ind + k, n)).wait_recv()
         rs_copy(k, ind).wait_send()
+        g_copy(k, ind).wait_send()
         return carry
 
     lax.fori_loop(1, n, drain, 0)
-    for b in range(n):
-        out_ref[:, b * w : (b + 1) * w] = unfold(ag[b].astype(jnp.float32)).astype(jnp.bfloat16)
-
-    def drain_ag(k, carry):
-        ag_copy(k, ind).wait_send()
-        return carry
-
-    lax.fori_loop(1, n, drain_ag, 0)
-
-    def drain_g(k, carry):
-        g_copy(k, gme).wait_send()
-        return carry
-
-    lax.fori_loop(1, group, drain_g, 0)
+    core_copy.wait_send()
     for c in range(CHUNKS):
         s_copy(c).wait_send()
         for k in range(1, ny):
             y_copy(k, c, y).wait_send()
+
+    def arrive(k, carry):
+        ag_copy(k, lax.rem(ind + k, n)).wait_recv()
+        return carry
+
+    lax.fori_loop(1, n, arrive, 0)
+    for b in range(n):
+        out_ref[:, b * w : (b + 1) * w] = unfold(ag[b].astype(jnp.float32)).astype(jnp.bfloat16)
+
+    def drain_ag(k, carry):
+        ag_copy(k, ind).wait_send()
+        return carry
+
+    lax.fori_loop(1, n, drain_ag, 0)
 
 
 def on_device(n, ny, genotype, probe, allele_mean, allele_scale):
@@ -319,7 +334,6 @@
     rank = probe.shape[0]
     w = cols // n
     ci = word_rows // (2 * CHUNKS) * PLANES
-    group = n * CORES
     f32, b16 = jnp.float32, jnp.bfloat16
     dma = pltpu.SemaphoreType.DMA
     vmem = pl.BlockSpec(memory_space=pltpu.VMEM)
@@ -343,7 +357,7 @@
             pltpu.VMEM((CHUNKS, 2 * rank, ci // 2), b16),
             pltpu.VMEM((CHUNKS, 2 * rank, ci // 2), b16),
             pltpu.VMEM((rank, CHUNKS * ci), b16),
-            pltpu.VMEM((group, 8, 128), f32),
+            pltpu.VMEM((n, 8, 128), f32),
             pltpu.VMEM((n, rank, w), f32),
             pltpu.VMEM((n, 2 * rank, w // 2), b16),
             pltpu.VMEM((n, 2 * rank, w // 2), b16),
@@ -353,7 +367,7 @@
             dma, dma,
             dma((ny, CHUNKS)), dma((ny, CHUNKS)),
             dma((CHUNKS,)), dma((CHUNKS,)),
-            dma((group,)), dma((group,)),
+            dma((n,)), dma((n,)),
             dma((n,)), dma((n,)),
             dma((n,)), dma((n,)),
         ],

time: 26.7 us -> 26.2 us (0.981)
  Pallas kernels: 25 us -> 24.5 us
    pallas_call x1, Pallas kernels: 25 us -> 24.5 us  [on_device(): pl.pallas_call(functools.partial(kernel, n, ny), out_shape=jax.ShapeDtype...]
where the time goes in v4:
time: 26.2 us; the launch traced here: 26.1 us
  Pallas kernels  24.5 us (94%)
  other arithmetic  1.58 us (6%)
    pallas_call x1, Pallas kernels, on_device(): pl.pallas_call(functools.partial(kernel, n, ny), out_shape=jax.ShapeDtype...  24.5 us
    convert_element_type x1, other arithmetic, on_device(): return pl.pallas_call(functools.partial(kernel, n, ny), out_shape=jax.Sha...  1.58 us

profile of v4, /device:TPU:0, one launch (start us, length us, event | category | flops | bytes accessed | tf_op | source)
XLA Modules:
  0.0 26.1 jit_solution(3254678867276764728)
XLA Ops:
  0.0 24.5 %shard_map.46 = bf16[24,2048]{1,0:T(8,128)(2,1)} custom-call(s32[512,2048]{1,0:T(8,128)} %g_hbm.1, bf16[24,2048]{1,0:T(8,128)(2,1)} %probe_hbm.1, f32[1,2048]{1,0:T(1,128)} %bitcast.2, f32[1,2048]{1,0:T(1,128)} %bitcast.3), custom_call_target="tpu_custom_call" | custom-call | flops 402653184 | bytes 4194304 | tf_op jit(solution)/shard_map/pallas_call | solution.py:340
  24.5 1.6 %convert_element_type.3 = f32[24,2048]{1,0:T(8,128)} convert(bf16[24,2048]{1,0:T(8,128)(2,1)} %shard_map.46) | non-fusion elementwise | flops 49152 | bytes 294912 | tf_op jit(solution)/shard_map/convert_element_type | solution.py:382

commit v5 on v4

--- a/solution.py
+++ b/solution.py
@@ -11,7 +11,7 @@
 CORES = 2
 CHUNKS = 4
 PLANES = 4
-SUBS = 2
+SUBS = 1
 
 
 def fold(x):
@@ -114,9 +114,9 @@
     scaled = probe_ref[...].astype(jnp.float32) * scale
     const = jnp.sum(scaled * mean, axis=1, keepdims=True)
     high = scaled.astype(jnp.bfloat16).astype(jnp.float32)
-    both = jnp.concatenate([high, scaled - high], axis=0).T.astype(jnp.bfloat16)
+    both = jnp.concatenate([high, scaled - high], axis=0).astype(jnp.bfloat16)
     for b in range(n):
-        weights[b] = both[b * w : (b + 1) * w, :]
+        weights[b] = both[:, b * w : (b + 1) * w]
         means[b] = mean[:, b * w : (b + 1) * w]
         scales[b] = scale[:, b * w : (b + 1) * w]
 
@@ -131,7 +131,7 @@
         at = pl.multiple_of(c * cw, 8)
         pieces = []
         for sub in range(SUBS):
-            total = jnp.zeros((si, 2 * rank), jnp.float32)
+            total = jnp.zeros((2 * rank, si), jnp.float32)
             for b in range(n):
                 packed = words[pl.ds(at + sub * sw, sw), b * w : (b + 1) * w]
                 tile = jnp.concatenate(
@@ -142,8 +142,8 @@
                     axis=0,
                 )
                 codes[b, pl.ds(pl.multiple_of(c * ci + sub * si, 16), si), :] = tile
-                total += jnp.dot(tile, weights[b], preferred_element_type=jnp.float32)
-            pieces.append(total.T)
+                total += dot_nt(weights[b], tile)
+            pieces.append(total)
         total = jnp.concatenate(pieces, axis=1)
         return (total[:rank] + total[rank:]) * plane_scale - const
 
@@ -337,6 +337,7 @@
     f32, b16 = jnp.float32, jnp.bfloat16
     dma = pltpu.SemaphoreType.DMA
     vmem = pl.BlockSpec(memory_space=pltpu.VMEM)
+    operands = genotype, probe, allele_mean.reshape(1, cols), allele_scale.reshape(1, cols)
     return pl.pallas_call(
         functools.partial(kernel, n, ny),
         out_shape=jax.ShapeDtypeStruct((rank, cols), b16),
@@ -348,7 +349,7 @@
             pltpu.VMEM((1, cols), f32),
             pltpu.VMEM((1, cols), f32),
             pltpu.VMEM((n, PLANES * word_rows, w), b16),
-            pltpu.VMEM((n, w, 2 * rank), b16),
+            pltpu.VMEM((n, 2 * rank, w), b16),
             pltpu.VMEM((n, 1, w), f32),
             pltpu.VMEM((n, 1, w), f32),
             pltpu.VMEM((2 * CHUNKS, rank, ci), f32),
@@ -372,14 +373,14 @@
             dma((n,)), dma((n,)),
         ],
         compiler_params=pltpu.CompilerParams(
-            collective_id=0, has_side_effects=True, vmem_limit_bytes=63 * 1024 * 1024
+            collective_id=0, has_side_effects=True, vmem_limit_bytes=48 * 1024 * 1024
         ),
         cost_estimate=pl.CostEstimate(
             flops=4 * rank * PLANES * word_rows * cols,
             bytes_accessed=4 * word_rows * cols,
             transcendentals=0,
         ),
-    )(genotype, probe, allele_mean.reshape(1, cols), allele_scale.reshape(1, cols)).astype(f32)
+    )(*[pltpu.with_memory_space_constraint(x, pltpu.HBM) for x in operands]).astype(f32)
 
 
 def solution(mesh):

time: 26.2 us -> 24.2 us (0.924)
  Pallas kernels: 24.5 us -> 23.4 us
  other arithmetic: 1.58 us -> 0.69 us
    pallas_call x1, Pallas kernels: 24.5 us -> 23.4 us  [on_device(): pl.pallas_call(functools.partial(kernel, n, ny), out_shape=jax.ShapeDtype...]
    convert_element_type x1, other arithmetic: 1.58 us -> 0.69 us  [on_device(): return pl.pallas_call(functools.partial(kernel, n, ny), out_shape=jax.Sha...]
where the time goes in v5:
time: 24.2 us; the launch traced here: 24.1 us
  Pallas kernels  23.4 us (97%)
  other arithmetic  0.69 us (3%)
    pallas_call x1, Pallas kernels, on_device(): pl.pallas_call(functools.partial(kernel, n, ny), out_shape=jax.ShapeDtype...  23.4 us
    convert_element_type x1, other arithmetic, on_device(): return pl.pallas_call(functools.partial(kernel, n, ny), out_shape=jax.Sha...  0.69 us

profile of v5, /device:TPU:0, one launch (start us, length us, event | category | flops | bytes accessed | tf_op | source)
XLA Modules:
  0.0 24.1 jit_solution(7872944436586090066)
XLA Ops:
  0.0 23.4 %shard_map.46 = bf16[24,2048]{1,0:T(8,128)(2,1)S(1)} custom-call(s32[512,2048]{1,0:T(8,128)} %g_hbm.1, bf16[24,2048]{1,0:T(8,128)(2,1)} %probe_hbm.1, f32[1,2048]{1,0:T(1,128)} %bitcast.2, f32[1,2048]{1,0:T(1,128)} %bitcast.3), custom_call_target="tpu_custom_call" | custom-call | flops 402653184 | bytes 4194304 | tf_op jit(solution)/shard_map/pallas_call | solution.py:341
  23.4 0.7 %convert_element_type.3 = f32[24,2048]{1,0:T(8,128)} convert(bf16[24,2048]{1,0:T(8,128)(2,1)S(1)} %shard_map.46) | non-fusion elementwise | flops 49152 | bytes 294912 | tf_op jit(solution)/shard_map/convert_element_type | solution.py:383

commit v6 on v5

--- a/solution.py
+++ b/solution.py
@@ -147,10 +147,12 @@
         total = jnp.concatenate(pieces, axis=1)
         return (total[:rank] + total[rank:]) * plane_scale - const
 
-    core_copy = pltpu.make_async_remote_copy(
-        src_ref=sk.at[0:CHUNKS], dst_ref=rx_core, send_sem=core_send, recv_sem=core_recv,
-        device_id=(ind, other), device_id_type=MESH,
-    )
+    def core_copy(c):
+        return pltpu.make_async_remote_copy(
+            src_ref=sk.at[c], dst_ref=rx_core.at[c], send_sem=core_send.at[c],
+            recv_sem=core_recv.at[c], device_id=(ind, other), device_id_type=MESH,
+        )
+
     def y_copy(k, c, slot):
         return pltpu.make_async_remote_copy(
             src_ref=ry.at[y, c], dst_ref=ry.at[slot, c],
@@ -161,18 +163,18 @@
     def chunk(c, carry):
         sk[c] = sketch_chunk(c)
 
-        @pl.when(c == CHUNKS - 1)
+        @pl.when(c == 0)
         def _():
             pl.semaphore_wait(barrier, n - 1 + 1 + ny - 1)
-            core_copy.start()
-
-        @pl.when(c == CHUNKS)
+
+        @pl.when(c < CHUNKS)
         def _():
-            core_copy.wait_recv()
+            core_copy(c).start()
 
         @pl.when(c >= CHUNKS)
         def _():
             j = c - CHUNKS
+            core_copy(j).wait_recv()
             ry[y, j] = fold(sk[c] + rx_core[j]).astype(jnp.bfloat16)
             for k in range(1, ny):
                 y_copy(k, j, y).start()
@@ -226,14 +228,26 @@
         0, CHUNKS, own_half,
         (jnp.zeros((rank, rank), jnp.float32), jnp.zeros((rank, 1), jnp.float32)),
     )
-    theirs = []
-    for c in range(CHUNKS):
+
+    def their_piece(c, gram, row_sum):
         s_copy(c).wait_recv()
-        theirs.append(unfold(s_in[c].astype(jnp.float32)))
-    theirs = jnp.concatenate(theirs, axis=1)
-    row_sum = row_sum + jnp.sum(theirs, axis=1, keepdims=True)
-    exact = theirs.astype(jnp.bfloat16)
-    gram = gram + dot_nt(exact, exact)
+        piece = unfold(s_in[c].astype(jnp.float32))
+        exact = piece.astype(jnp.bfloat16)
+        row_sum = row_sum + jnp.sum(piece, axis=1, keepdims=True)
+        return (piece * plane_scale).astype(jnp.bfloat16), gram + dot_nt(exact, exact), row_sum
+
+    def their_half(c, carry):
+        piece, gram, row_sum = their_piece(c, *carry)
+        at = pl.multiple_of(c * ci, 16)
+        for b in range(n):
+            qacc[b] += jnp.dot(
+                piece, codes[b, pl.ds(at, ci), :], preferred_element_type=jnp.float32
+            )
+        return gram, row_sum
+
+    gram, row_sum = lax.fori_loop(0, CHUNKS - 1, their_half, (gram, row_sum))
+    last, gram, row_sum = their_piece(CHUNKS - 1, gram, row_sum)
+    s_cat[...] = last
     pad = jnp.zeros((8, 32 - rank), jnp.float32)
     parts = []
     for g in range(rank // 8):
@@ -241,7 +255,6 @@
     parts.append(jnp.zeros((8, 128 - 4 * rank), jnp.float32))
     rg[ind] = jnp.concatenate(parts, axis=1)
     lax.fori_loop(1, n, g_start, 0)
-    s_cat[...] = (theirs * jnp.concatenate([plane_scale] * CHUNKS, axis=1)).astype(jnp.bfloat16)
 
     def rs_copy(k, slot):
         to = lax.rem(ind + k, n)
@@ -254,7 +267,7 @@
     def product(k, carry):
         b = lax.rem(ind + k, n)
         q = qacc[b] + jnp.dot(
-            s_cat[...], codes[b, 0:span, :], preferred_element_type=jnp.float32
+            s_cat[...], codes[b, span - ci : span, :], preferred_element_type=jnp.float32
         )
         rs_out[b] = fold(scales[b] * (q - means[b] * row_sum)).astype(jnp.bfloat16)
 
@@ -308,18 +321,17 @@
         return carry
 
     lax.fori_loop(1, n, drain, 0)
-    core_copy.wait_send()
     for c in range(CHUNKS):
+        core_copy(c).wait_send()
         s_copy(c).wait_send()
         for k in range(1, ny):
             y_copy(k, c, y).wait_send()
 
-    def arrive(k, carry):
-        ag_copy(k, lax.rem(ind + k, n)).wait_recv()
-        return carry
-
-    lax.fori_loop(1, n, arrive, 0)
     for b in range(n):
+        @pl.when(ind != b)
+        def _():
+            ag_copy(1, b).wait_recv()
+
         out_ref[:, b * w : (b + 1) * w] = unfold(ag[b].astype(jnp.float32)).astype(jnp.bfloat16)
 
     def drain_ag(k, carry):
@@ -357,7 +369,7 @@
             pltpu.VMEM((ny, CHUNKS, 2 * rank, ci // 2), b16),
             pltpu.VMEM((CHUNKS, 2 * rank, ci // 2), b16),
             pltpu.VMEM((CHUNKS, 2 * rank, ci // 2), b16),
-            pltpu.VMEM((rank, CHUNKS * ci), b16),
+            pltpu.VMEM((rank, ci), b16),
             pltpu.VMEM((n, 8, 128), f32),
             pltpu.VMEM((n, rank, w), f32),
             pltpu.VMEM((n, 2 * rank, w // 2), b16),
@@ -365,7 +377,7 @@
             pltpu.VMEM((n, 2 * rank, w // 2), b16),
             dma((2 * CHUNKS,)),
             dma((3,)),
-            dma, dma,
+            dma((CHUNKS,)), dma((CHUNKS,)),
             dma((ny, CHUNKS)), dma((ny, CHUNKS)),
             dma((CHUNKS,)), dma((CHUNKS,)),
             dma((n,)), dma((n,)),

time: 24.2 us -> 25.1 us (1.037)
  Pallas kernels: 23.4 us -> 24.3 us
    pallas_call x1, Pallas kernels: 23.4 us -> 24.3 us  [on_device(): pl.pallas_call(functools.partial(kernel, n, ny), out_shape=jax.ShapeDtype...]
where the time goes in v6:
time: 25.1 us; the launch traced here: 25 us
  Pallas kernels  24.3 us (97%)
  other arithmetic  0.69 us (3%)
    pallas_call x1, Pallas kernels, on_device(): pl.pallas_call(functools.partial(kernel, n, ny), out_shape=jax.ShapeDtype...  24.3 us
    convert_element_type x1, other arithmetic, on_device(): return pl.pallas_call(functools.partial(kernel, n, ny), out_shape=jax.Sha...  0.69 us

profile of v6, /device:TPU:0, one launch (start us, length us, event | category | flops | bytes accessed | tf_op | source)
XLA Modules:
  0.0 25.0 jit_solution(16737442978399308914)
XLA Ops:
  0.0 24.3 %shard_map.46 = bf16[24,2048]{1,0:T(8,128)(2,1)S(1)} custom-call(s32[512,2048]{1,0:T(8,128)} %g_hbm.1, bf16[24,2048]{1,0:T(8,128)(2,1)} %probe_hbm.1, f32[1,2048]{1,0:T(1,128)} %bitcast.2, f32[1,2048]{1,0:T(1,128)} %bitcast.3), custom_call_target="tpu_custom_call" | custom-call | flops 402653184 | bytes 4194304 | tf_op jit(solution)/shard_map/pallas_call | solution.py:353
  24.3 0.7 %convert_element_type.3 = f32[24,2048]{1,0:T(8,128)} convert(bf16[24,2048]{1,0:T(8,128)(2,1)S(1)} %shard_map.46) | non-fusion elementwise | flops 49152 | bytes 294912 | tf_op jit(solution)/shard_map/convert_element_type | solution.py:395

commit v7 on v6

--- a/solution.py
+++ b/solution.py
@@ -228,26 +228,14 @@
         0, CHUNKS, own_half,
         (jnp.zeros((rank, rank), jnp.float32), jnp.zeros((rank, 1), jnp.float32)),
     )
-
-    def their_piece(c, gram, row_sum):
+    theirs = []
+    for c in range(CHUNKS):
         s_copy(c).wait_recv()
-        piece = unfold(s_in[c].astype(jnp.float32))
-        exact = piece.astype(jnp.bfloat16)
-        row_sum = row_sum + jnp.sum(piece, axis=1, keepdims=True)
-        return (piece * plane_scale).astype(jnp.bfloat16), gram + dot_nt(exact, exact), row_sum
-
-    def their_half(c, carry):
-        piece, gram, row_sum = their_piece(c, *carry)
-        at = pl.multiple_of(c * ci, 16)
-        for b in range(n):
-            qacc[b] += jnp.dot(
-                piece, codes[b, pl.ds(at, ci), :], preferred_element_type=jnp.float32
-            )
-        return gram, row_sum
-
-    gram, row_sum = lax.fori_loop(0, CHUNKS - 1, their_half, (gram, row_sum))
-    last, gram, row_sum = their_piece(CHUNKS - 1, gram, row_sum)
-    s_cat[...] = last
+        theirs.append(unfold(s_in[c].astype(jnp.float32)))
+    theirs = jnp.concatenate(theirs, axis=1)
+    row_sum = row_sum + jnp.sum(theirs, axis=1, keepdims=True)
+    exact = theirs.astype(jnp.bfloat16)
+    gram = gram + dot_nt(exact, exact)
     pad = jnp.zeros((8, 32 - rank), jnp.float32)
     parts = []
     for g in range(rank // 8):
@@ -255,6 +243,7 @@
     parts.append(jnp.zeros((8, 128 - 4 * rank), jnp.float32))
     rg[ind] = jnp.concatenate(parts, axis=1)
     lax.fori_loop(1, n, g_start, 0)
+    s_cat[...] = (theirs * jnp.concatenate([plane_scale] * CHUNKS, axis=1)).astype(jnp.bfloat16)
 
     def rs_copy(k, slot):
         to = lax.rem(ind + k, n)
@@ -267,7 +256,7 @@
     def product(k, carry):
         b = lax.rem(ind + k, n)
         q = qacc[b] + jnp.dot(
-            s_cat[...], codes[b, span - ci : span, :], preferred_element_type=jnp.float32
+            s_cat[...], codes[b, 0:span, :], preferred_element_type=jnp.float32
         )
         rs_out[b] = fold(scales[b] * (q - means[b] * row_sum)).astype(jnp.bfloat16)
 
@@ -369,7 +358,7 @@
             pltpu.VMEM((ny, CHUNKS, 2 * rank, ci // 2), b16),
             pltpu.VMEM((CHUNKS, 2 * rank, ci // 2), b16),
             pltpu.VMEM((CHUNKS, 2 * rank, ci // 2), b16),
-            pltpu.VMEM((rank, ci), b16),
+            pltpu.VMEM((rank, CHUNKS * ci), b16),
             pltpu.VMEM((n, 8, 128), f32),
             pltpu.VMEM((n, rank, w), f32),
             pltpu.VMEM((n, 2 * rank, w // 2), b16),

time: 25.1 us -> 24.8 us (0.988)
  Pallas kernels: 24.3 us -> 24 us
    pallas_call x1, Pallas kernels: 24.3 us -> 24 us  [on_device(): pl.pallas_call(functools.partial(kernel, n, ny), out_shape=jax.ShapeDtype...]
where the time goes in v7:
time: 24.8 us; the launch traced here: 24.7 us
  Pallas kernels  24 us (97%)
  other arithmetic  0.69 us (3%)
    pallas_call x1, Pallas kernels, on_device(): pl.pallas_call(functools.partial(kernel, n, ny), out_shape=jax.ShapeDtype...  24 us
    convert_element_type x1, other arithmetic, on_device(): return pl.pallas_call(functools.partial(kernel, n, ny), out_shape=jax.Sha...  0.69 us

profile of v7, /device:TPU:0, one launch (start us, length us, event | category | flops | bytes accessed | tf_op | source)
XLA Modules:
  0.0 24.7 jit_solution(3125160179565146287)
XLA Ops:
  0.0 24.0 %shard_map.46 = bf16[24,2048]{1,0:T(8,128)(2,1)S(1)} custom-call(s32[512,2048]{1,0:T(8,128)} %g_hbm.1, bf16[24,2048]{1,0:T(8,128)(2,1)} %probe_hbm.1, f32[1,2048]{1,0:T(1,128)} %bitcast.2, f32[1,2048]{1,0:T(1,128)} %bitcast.3), custom_call_target="tpu_custom_call" | custom-call | flops 402653184 | bytes 4194304 | tf_op jit(solution)/shard_map/pallas_call | solution.py:342
  24.0 0.7 %convert_element_type.3 = f32[24,2048]{1,0:T(8,128)} convert(bf16[24,2048]{1,0:T(8,128)(2,1)S(1)} %shard_map.46) | non-fusion elementwise | flops 49152 | bytes 294912 | tf_op jit(solution)/shard_map/convert_element_type | solution.py:384
